TPU v7x, 128 devices: a whole 4x4x4 slice. The times are simulated.
128 devices in a mesh: ty: 8 (over z_hi, x), tx: 16 (over y, z_lo, core).
Axes of the slice: x: 4, y: 4, z: 4 (z_hi: 2, z_lo: 2; z = z_hi * 2 + z_lo), core: 2. Of those that a mesh axis runs over, the one named last changes fastest.
Arguments:
- object_slab: float32 [2, 2, 4096, 8192], P(None, None, 'ty', 'tx'), may hold values from -4 to 4
- probe_wave: float32 [2, 256, 256], replicated, may hold values from -5 to 5
- frames: float32 [768, 256, 256], P('tx'), may hold values from 0.05 to 8
- scan_tiles: int32 [768], replicated, may hold values from 0 to 127, as said below
- scan_offsets: int32 [768, 2], replicated, may hold values from 0 to 511, as said below
Outputs:
- new_object: float32 [2, 2, 4096, 8192], P(None, None, 'ty', 'tx')
- new_probe: float32 [2, 256, 256], replicated
Inputs may be any that keep to these rules, and one draw needn't show every extreme that they name: `scan_tiles`: tiles are numbered row by row: tile row times 16 plus tile column. Every tile is named by at most 8 scan positions, and some tile by exactly 8. Within the frames of one owner (aligned blocks of 48 positions) no tile is named twice. `scan_offsets`: row offsets lie in 0 to 511 and column offsets in 0 to 511; windows may reach past the tile's lower and right edges.
All inputs are finite; a program needn't handle non-finite values.
Results may differ from a plain program's by a relative error of at most 0.0003.
Values sent between devices are 32-bit elements; how exact they have to be, the bound alone decides.
A program may use at most 192 MiB of HBM per device.

v0:
```python
import math

import jax
import jax.numpy as jnp
from jax import lax
from jax.sharding import PartitionSpec as P

TILE_CAP = 8


BACKGROUND = 0.5
FRESNEL = 0.25
OBJECT_RATE = 0.25
PROBE_RATE = 4.0


def passed_along(value, axis, steps):
    count = lax.axis_size(axis)
    leading, last = (max(0, -steps), min(count, count - steps))
    return lax.ppermute(value, axis, [(source, source + steps) for source in range(leading, last)])


def kernel_phase(points):
    indices = jnp.arange(points, dtype=jnp.int32)
    frequency = (indices + points // 2) % points - points // 2
    square = (frequency * frequency).astype(jnp.float32)
    return -jnp.pi * FRESNEL / points * (square[:, None] + square[None, :])


def fourier_tables(points):
    indices = jnp.arange(points, dtype=jnp.int32)
    product = indices[:, None] * indices[None, :] % points
    angles = 2.0 * jnp.pi / points * product.astype(jnp.float32)
    factor = 1.0 / math.sqrt(points)
    return (jnp.cos(angles) * factor, -jnp.sin(angles) * factor)


def apply_left(table, stack):
    return jnp.einsum("kn,bnm->bkm", table, stack, precision=lax.Precision.HIGHEST)


def apply_right(stack, table):
    return jnp.einsum("bnm,mk->bnk", stack, table, precision=lax.Precision.HIGHEST)


def transform(real_part, imag_part, table_re, table_im):
    mid_re = apply_left(table_re, real_part) - apply_left(table_im, imag_part)
    mid_im = apply_left(table_re, imag_part) + apply_left(table_im, real_part)
    out_re = apply_right(mid_re, table_re) - apply_right(mid_im, table_im)
    out_im = apply_right(mid_re, table_im) + apply_right(mid_im, table_re)
    return (out_re, out_im)


def slot_losses(windows, probe_now, measured, weights, tables):
    table_re, table_im, kernel_re, kernel_im = tables
    probe_re = probe_now[0][None]
    probe_im = probe_now[1][None]
    win_re = windows[:, 0, 0]
    win_im = windows[:, 0, 1]
    wave_re = probe_re * win_re - probe_im * win_im
    wave_im = probe_re * win_im + probe_im * win_re
    spec_re, spec_im = transform(wave_re, wave_im, table_re, table_im)
    turned_re = kernel_re * spec_re - kernel_im * spec_im
    turned_im = kernel_re * spec_im + kernel_im * spec_re
    back_re, back_im = transform(turned_re, turned_im, table_re, -table_im)
    win_re = windows[:, 1, 0]
    win_im = windows[:, 1, 1]
    wave_re = back_re * win_re - back_im * win_im
    wave_im = back_re * win_im + back_im * win_re
    far_re, far_im = transform(wave_re, wave_im, table_re, table_im)
    model_amp = jnp.sqrt(far_re * far_re + far_im * far_im + BACKGROUND)
    target = jnp.sqrt(measured + BACKGROUND)
    return jnp.sum(weights[:, None, None] * (model_amp - target) ** 2)


def local(object_slab, probe_wave, frames, scan_tiles, scan_offsets):
    columns = lax.axis_size("tx")
    row_index = lax.axis_index("ty")
    col_index = lax.axis_index("tx")
    owned = frames.shape[0]
    points = probe_wave.shape[-1]
    layers = object_slab.shape[0]
    tile_rows = object_slab.shape[2]
    tile_cols = object_slab.shape[3]
    capacity = TILE_CAP
    total_frames = owned * columns
    my_tile = row_index * columns + col_index
    by_owner = scan_tiles.reshape(columns, owned)
    mine = lax.dynamic_index_in_dim(by_owner, col_index, 0, keepdims=False)
    wanted = row_index * columns + jnp.arange(columns, dtype=jnp.int32)
    pick = (mine[None, :] == wanted[:, None]).astype(jnp.float32)
    outgoing = jnp.einsum("bi,ipq->bpq", pick, frames, precision=lax.Precision.HIGHEST)
    arrived = lax.all_to_all(outgoing, "tx", split_axis=0, concat_axis=0, tiled=True)
    matches = by_owner == my_tile
    present = jnp.any(matches, axis=1)
    which = jnp.sum(matches.astype(jnp.int32) * jnp.arange(owned, dtype=jnp.int32)[None, :], axis=1)
    global_ids = jnp.arange(columns, dtype=jnp.int32) * owned + which
    ranks = jnp.cumsum(present.astype(jnp.int32)) - 1
    slot_pick = present[None, :] & (
        ranks[None, :] == jnp.arange(capacity, dtype=jnp.int32)[:, None]
    )
    slot_float = slot_pick.astype(jnp.float32)
    measured = jnp.einsum("kj,jpq->kpq", slot_float, arrived, precision=lax.Precision.HIGHEST)
    weights = jnp.sum(slot_float, axis=1)
    chosen_ids = jnp.sum(slot_pick.astype(jnp.int32) * global_ids[None, :], axis=1)
    slot_offsets = scan_offsets[chosen_ids]
    table_re, table_im = fourier_tables(points)
    phases = kernel_phase(points)
    tables = (table_re, table_im, jnp.cos(phases)[None], jnp.sin(phases)[None])
    slab_now = object_slab
    probe_now = probe_wave
    right_part = passed_along(slab_now[:, :, :, :points], "tx", -1)
    wide = jnp.concatenate([slab_now, right_part], axis=3)
    lower_part = passed_along(wide[:, :, :points, :], "ty", -1)
    extended = jnp.concatenate([wide, lower_part], axis=2)
    pieces = []
    for slot in range(capacity):
        anchor = (jnp.int32(0), jnp.int32(0), slot_offsets[slot, 0], slot_offsets[slot, 1])
        pieces.append(lax.dynamic_slice(extended, anchor, (layers, 2, points, points)))
    windows = jnp.stack(pieces, axis=0)

    def local_loss(window_stack, probe_value):
        return slot_losses(window_stack, probe_value, measured, weights, tables)

    unused, pullback = jax.vjp(local_loss, windows, probe_now)
    grad_windows, grad_probe = pullback(jnp.ones((), jnp.float32))
    grad_extended = jnp.zeros_like(extended)
    for slot in range(capacity):
        anchor = (jnp.int32(0), jnp.int32(0), slot_offsets[slot, 0], slot_offsets[slot, 1])
        existing = lax.dynamic_slice(grad_extended, anchor, (layers, 2, points, points))
        grad_extended = lax.dynamic_update_slice(
            grad_extended, existing + grad_windows[slot], anchor
        )
    lower_back = passed_along(grad_extended[:, :, tile_rows:, :], "ty", 1)
    wide_grad = grad_extended[:, :, :tile_rows, :].at[:, :, :points, :].add(lower_back)
    right_back = passed_along(wide_grad[:, :, :, tile_cols:], "tx", 1)
    grad_tile = wide_grad[:, :, :, :tile_cols].at[:, :, :, :points].add(right_back)
    probe_sum = lax.psum(grad_probe, ("ty", "tx"))
    slab_now = slab_now - OBJECT_RATE * grad_tile
    probe_now = probe_now - PROBE_RATE / total_frames * probe_sum
    return (slab_now, probe_now)


def solution(mesh):
    return jax.shard_map(
        local,
        mesh=mesh,
        in_specs=(P(None, None, "ty", "tx"), P(), P("tx", None, None), P(), P()),
        out_specs=(P(None, None, "ty", "tx"), P()),
        check_vma=False,
    )
```

profile of v0, /device:TPU:1, one launch (start us, length us, event | category | flops | bytes accessed | tf_op | source)
XLA Modules:
  0.0 739.8 jit_solution(7737122343783004010)
XLA Ops:
  13.7 15.5 %fusion = f32[16,256,256]{2,0,1:T(8,128)S(1)} fusion(f32[48,256,256]{2,1,0:T(8,128)} %param.11, s32[48]{0:T(128)S(1)} %fusion.295, s32[16]{0:T(128)S(1)} %iota_add_fusion), kind=kOutput, calls=%fused_computation.17 | convolution fusion | flops 603980544 | bytes 16777472 | tf_op jit(solution)/shard_map/bi,ipq->bpq/dot_general | solution.py:92
  33.6 6.0 all-to-all-start
  85.8 6.5 all-to-all-done
  92.3 6.1 fusion.2
  98.5 19.2 %collective-permute-done.1 = f32[2,2,256,768]{3,2,1,0:T(8,128)S(1)} collective-permute-done((f32[2,2,256,768]{3,2,1,0:T(8,128)}, f32[2,2,256,768]{3,2,1,0:T(8,128)S(1)}, u32[]{:S(2)}, u32[]{:S(2)}) %collective-permute-start.1) | collective-permute-done | bytes 3145760 | tf_op jit(solution)/shard_map/ppermute | solution.py:20
  123.2 4.8 fusion.218
  128.0 4.5 fusion.215
  137.0 4.8 fusion.59
  150.6 4.6 fusion.89
  159.7 4.8 fusion.155
  173.5 4.8 fusion.53
  187.3 4.6 fusion.92
  191.9 6.3 multiply_subtract_fusion.1
  198.1 4.7 fusion.208
  207.2 4.5 convolution_add_fusion.3
  211.8 4.8 fusion.43
  221.0 4.5 convolution_subtract_fusion
  225.5 4.7 fusion.101
  230.3 6.5 fusion.70
  263.9 6.4 fusion.34
  270.3 4.7 fusion.198
  318.0 5.0 multiply_reduce_fusion
  331.6 12.4 %dynamic_update_slice.24 = f32[2,2,768,768]{3,2,1,0:T(8,128)} dynamic-update-slice(f32[2,2,768,768]{3,2,1,0:T(8,128)} %broadcast_in_dim.10, f32[2,2,256,256]{3,2,1,0:T(8,128)S(1)} %slice_bitcast_fusion.11, s32[]{:T(128)} %constant.110.clone.1, s32[]{:T(128)} %constant.110.clone.1, s32[]{:T(128)S(6)} %select_n.223, s32[]{:T(128)S(6)} %select_n.224) | dynamic-update-slice | bytes 2097156 | tf_op jit(solution)/shard_map/dynamic_update_slice | solution.py:131
  346.1 11.8 %dynamic_update_slice.25 = f32[2,2,768,768]{3,2,1,0:T(8,128)} dynamic-update-slice(f32[2,2,768,768]{3,2,1,0:T(8,128)} %dynamic_update_slice.24, f32[2,2,256,256]{3,2,1,0:T(8,128)S(1)} %fusion.152, s32[]{:T(128)} %constant.110.clone.1, s32[]{:T(128)} %constant.110.clone.1, s32[]{:T(128)S(6)} %select_n.225, s32[]{:T(128)S(6)} %select_n.226) | dynamic-update-slice | bytes 2097156 | tf_op jit(solution)/shard_map/dynamic_update_slice | solution.py:131
  360.0 12.2 %dynamic_update_slice.26 = f32[2,2,768,768]{3,2,1,0:T(8,128)} dynamic-update-slice(f32[2,2,768,768]{3,2,1,0:T(8,128)} %dynamic_update_slice.25, f32[2,2,256,256]{3,2,1,0:T(8,128)S(1)} %fusion.151, s32[]{:T(128)} %constant.110.clone.1, s32[]{:T(128)} %constant.110.clone.1, s32[]{:T(128)S(6)} %select_n.227, s32[]{:T(128)S(6)} %select_n.228) | dynamic-update-slice | bytes 2097156 | tf_op jit(solution)/shard_map/dynamic_update_slice | solution.py:131
  374.4 12.4 %dynamic_update_slice.27 = f32[2,2,768,768]{3,2,1,0:T(8,128)} dynamic-update-slice(f32[2,2,768,768]{3,2,1,0:T(8,128)} %dynamic_update_slice.26, f32[2,2,256,256]{3,2,1,0:T(8,128)S(1)} %fusion.150, s32[]{:T(128)} %constant.110.clone.1, s32[]{:T(128)} %constant.110.clone.1, s32[]{:T(128)S(6)} %select_n.229, s32[]{:T(128)S(6)} %select_n.230) | dynamic-update-slice | bytes 2097156 | tf_op jit(solution)/shard_map/dynamic_update_slice | solution.py:131
  388.9 11.5 %dynamic_update_slice.28 = f32[2,2,768,768]{3,2,1,0:T(8,128)} dynamic-update-slice(f32[2,2,768,768]{3,2,1,0:T(8,128)} %dynamic_update_slice.27, f32[2,2,256,256]{3,2,1,0:T(8,128)S(1)} %fusion.149, s32[]{:T(128)} %constant.110.clone.1, s32[]{:T(128)} %constant.110.clone.1, s32[]{:T(128)S(6)} %select_n.231, s32[]{:T(128)S(6)} %select_n.232) | dynamic-update-slice | bytes 2097156 | tf_op jit(solution)/shard_map/dynamic_update_slice | solution.py:131
  402.5 12.0 %dynamic_update_slice.29 = f32[2,2,768,768]{3,2,1,0:T(8,128)} dynamic-update-slice(f32[2,2,768,768]{3,2,1,0:T(8,128)} %dynamic_update_slice.28, f32[2,2,256,256]{3,2,1,0:T(8,128)S(1)} %fusion.148, s32[]{:T(128)} %constant.110.clone.1, s32[]{:T(128)} %constant.110.clone.1, s32[]{:T(128)S(6)} %select_n.233, s32[]{:T(128)S(6)} %select_n.234) | dynamic-update-slice | bytes 2097156 | tf_op jit(solution)/shard_map/dynamic_update_slice | solution.py:131
  416.6 12.2 %dynamic_update_slice.30 = f32[2,2,768,768]{3,2,1,0:T(8,128)} dynamic-update-slice(f32[2,2,768,768]{3,2,1,0:T(8,128)} %dynamic_update_slice.29, f32[2,2,256,256]{3,2,1,0:T(8,128)S(1)} %fusion.147, s32[]{:T(128)} %constant.110.clone.1, s32[]{:T(128)} %constant.110.clone.1, s32[]{:T(128)S(6)} %select_n.235, s32[]{:T(128)S(6)} %select_n.236) | dynamic-update-slice | bytes 2097156 | tf_op jit(solution)/shard_map/dynamic_update_slice | solution.py:131
  430.9 12.4 %dynamic_update_slice.31 = f32[2,2,768,768]{3,2,1,0:T(8,128)} dynamic-update-slice(f32[2,2,768,768]{3,2,1,0:T(8,128)} %dynamic_update_slice.30, f32[2,2,256,256]{3,2,1,0:T(8,128)S(1)} %fusion.146, s32[]{:T(128)} %constant.110.clone.1, s32[]{:T(128)} %constant.110.clone.1, s32[]{:T(128)S(6)} %select_n.237, s32[]{:T(128)S(6)} %select_n.238) | dynamic-update-slice | bytes 2097156 | tf_op jit(solution)/shard_map/dynamic_update_slice | solution.py:131
  452.2 63.8 %collective-permute-done.2 = f32[2,2,256,768]{3,2,1,0:T(8,128)S(1)} collective-permute-done((f32[2,2,256,768]{3,2,1,0:T(8,128)S(1)}, f32[2,2,256,768]{3,2,1,0:T(8,128)S(1)}, u32[]{:S(2)}, u32[]{:S(2)}) %collective-permute-start.2) | collective-permute-done | bytes 3145760 | tf_op jit(solution)/shard_map/ppermute | solution.py:20
  527.9 194.2 %all-reduce.8.cloned.1.call-done = f32[2,256,256]{2,1,0:T(8,128)} async-done(((f32[2,256,256]{2,1,0:T(8,128)}), f32[2,256,256]{2,1,0:T(8,128)}) %all-reduce.8.cloned.1.call-update) | async-done | bytes 524304 | tf_op jit(solution)/shard_map/psum | solution.py:138
  (130 shorter events, 201.7 us)
Async XLA Ops:
  7.2 6.4 copy-start.17
  10.2 32.1 %collective-permute-start = (f32[2,2,512,256]{3,2,1,0:T(8,128)}, f32[2,2,512,256]{3,2,1,0:T(8,128)S(1)}, u32[]{:S(2)}, u32[]{:S(2)}) collective-permute-start(f32[2,2,512,256]{3,2,1,0:T(8,128)} %slice.185), channel_id=1, source_target_pairs={{1,0},{2,1},{3,2},{4,3},{5,4},{6,5},{7,6},{8,7},{9,8},{10,9},{11,1... | collective-permute-start | bytes 6291464 | tf_op jit(solution)/shard_map/ppermute | solution.py:20
  33.6 58.8 %all-to-all-start = ((f32[16,256,256]{2,1,0:T(8,128)}), f32[16,256,256]{2,1,0:T(8,128)}, u32[]{:S(2)}, u32[]{:S(2)}) async-start(f32[16,256,256]{2,1,0:T(8,128)} %copy.150), calls=%async_computation | async-start | bytes 8388608 | tf_op jit(solution)/shard_map/all_to_all | solution.py:93
  39.6 682.5 %all-reduce.8.cloned.1.call-start = ((), (), s32[]{:S(2)}) async-start(), calls=%async_computation.1 | async-start | bytes 1048576 | tf_op jit(solution)/shard_map/psum | solution.py:138
  42.5 3.6 copy-start
  42.5 6.3 copy-start.15
  46.1 71.6 %collective-permute-start.1 = (f32[2,2,256,768]{3,2,1,0:T(8,128)}, f32[2,2,256,768]{3,2,1,0:T(8,128)S(1)}, u32[]{:S(2)}, u32[]{:S(2)}) collective-permute-start(f32[2,2,256,768]{3,2,1,0:T(8,128)} %slice.224), channel_id=1, source_target_pairs={{16,0},{32,16},{48,32},{64,48},{80,64},{96,80},{112,96},{17,1},{33... | collective-permute-start | bytes 9437192 | tf_op jit(solution)/shard_map/ppermute | solution.py:20
  48.1 0.5 copy-start.16
  92.3 25.4 %copy-start.1 = (f32[2,2,512,768]{3,2,1,0:T(8,128)S(1)}, f32[2,2,512,768]{3,2,1,0:T(8,128)}, u32[]{:S(2)}) copy-start(f32[2,2,512,768]{3,2,1,0:T(8,128)} %copy-done) | copy-start | bytes 18874372
  122.2 1.0 copy-start.7
  122.2 1.0 copy-start.9
  155.2 4.5 copy-start.5
  270.3 4.7 copy-start.6
  314.9 3.1 copy-start.8
  314.9 3.1 copy-start.10
  317.9 5.0 copy-start.11
  318.0 5.0 copy-start.12
  323.8 3.3 copy-start.3
  445.5 70.5 %collective-permute-start.2 = (f32[2,2,256,768]{3,2,1,0:T(8,128)S(1)}, f32[2,2,256,768]{3,2,1,0:T(8,128)S(1)}, u32[]{:S(2)}, u32[]{:S(2)}) collective-permute-start(f32[2,2,256,768]{3,2,1,0:T(8,128)S(1)} %slice.239), channel_id=1, source_target_pairs={{0,16},{16,32},{32,48},{48,64},{64,80},{80,96},{96,112},{1,17},{17... | collective-permute-start | bytes 9437192 | tf_op jit(solution)/shard_map/ppermute | solution.py:20
  518.5 2.6 copy-start.2
  521.1 5.8 copy-start.14
  522.6 199.5 %copy-start.13 = (f32[2,256,256]{2,1,0:T(8,128)S(1)}, f32[2,256,256]{2,1,0:T(8,128)}, u32[]{:S(2)}) copy-start(f32[2,256,256]{2,1,0:T(8,128)} %param.10) | copy-start | bytes 1572868
  522.6 204.0 %collective-permute-start.3 = (f32[2,2,512,256]{3,2,1,0:T(8,128)}, f32[2,2,512,256]{3,2,1,0:T(8,128)S(1)}, u32[]{:S(2)}, u32[]{:S(2)}) collective-permute-start(f32[2,2,512,256]{3,2,1,0:T(8,128)} %slice.242), channel_id=1, source_target_pairs={{0,1},{1,2},{2,3},{3,4},{4,5},{5,6},{6,7},{7,8},{8,9},{9,10},{10,1... | collective-permute-start | bytes 6291464 | tf_op jit(solution)/shard_map/ppermute | solution.py:20
  726.6 2.8 copy-start.4
Sparse Core Ops, SparseCore 0:
  528.0 194.0 all-reduce.7
where the time goes:
time: 752 us; the launch traced here: 740 us
  waiting for transfers between devices  284 us (38%)
  matrix products  215 us (29%)
  local copies, waits for them, and re-layouts  136 us (18%)
  between operations  44.6 us (6%)
  other arithmetic  42.4 us (6%)
  starting transfers between devices  18.4 us (2%)
    psum x1, waiting for transfers between devices, local(): probe_sum = lax.psum(grad_probe, ('ty', 'tx'))  194 us
    dynamic_update_slice x8, local copies, waits for them, and re-layouts, local(): lax.dynamic_update_slice(grad_extended, existing + grad_windows[slot], an...  96.9 us
    dot_general x24, matrix products, apply_left(): jnp.einsum('kn,bnm->bkm', table, stack, precision=lax.Precision.HIGHEST)  96.6 us
    dot_general x24, matrix products, apply_right(): jnp.einsum('bnm,mk->bnk', stack, table, precision=lax.Precision.HIGHEST)  96.3 us
    ppermute x4, waiting for transfers between devices, passed_along(): lax.ppermute(value, axis, [(source, source + steps) for source in range(l...  83 us
    dot_general x1, matrix products, local(): jnp.einsum('bi,ipq->bpq', pick, frames, precision=lax.Precision.HIGHEST)  15.5 us
  transfers between devices with their start and end apart: 6, of which 4 were waited for; matrix products, arithmetic and copies ran while one was open for 7% of the time, Pallas kernels for 0%

commit v1 on v0

v1 whole, which is shorter than its diff:
```python
import functools
import math

import jax
import jax.numpy as jnp
import ml_dtypes
import numpy as np
from jax import lax
from jax.experimental import pallas as pl
from jax.experimental.pallas import tpu as pltpu
from jax.sharding import PartitionSpec as P

MESH = pl.DeviceIdType.MESH
TILE_CAP = 8
BACKGROUND = 0.5
FRESNEL = 0.25
OBJECT_RATE = 0.25
PROBE_RATE = 4.0
VMEM_LIMIT = 56 * 1024 * 1024


def passed_along(value, axis, steps):
    count = lax.axis_size(axis)
    leading, last = (max(0, -steps), min(count, count - steps))
    return lax.ppermute(value, axis, [(source, source + steps) for source in range(leading, last)])


def real_form(matrix):
    return np.block([[matrix.real, -matrix.imag], [matrix.imag, matrix.real]])


def split_table(table):
    high = table.astype(ml_dtypes.bfloat16)
    low = (table - high.astype(np.float64)).astype(ml_dtypes.bfloat16)
    return high, low


def left_table(table):
    high, low = split_table(table)
    return np.concatenate([high, low, high], axis=1)


def right_table(table):
    high, low = split_table(table)
    return np.concatenate([high, low, high], axis=0)


def half_transforms(points):
    half = points // 2
    places = np.arange(half)
    even = np.exp(-2j * np.pi * ((2 * places[:, None]) * places[None, :] % points) / points)
    odd = np.exp(-2j * np.pi * ((2 * places[:, None] + 1) * places[None, :] % points) / points)
    return even / math.sqrt(points), odd / math.sqrt(points)


def build_tables(points):
    even, odd = half_transforms(points)
    places = np.arange(points)
    frequency = (places + points // 2) % points - points // 2
    phase = np.exp(-1j * np.pi * FRESNEL / points * frequency.astype(np.float64) ** 2)
    spread_even = even.conj().T @ (phase[0::2, None] * even)
    spread_odd = odd.conj().T @ (phase[1::2, None] * odd)
    spread = [real_form(spread_even), real_form(spread_odd)]
    fourier = [real_form(even), real_form(odd)]
    order = np.concatenate([places[0::2], places[1::2]])
    shuffle = (places[:, None] == order[None, :]).astype(ml_dtypes.bfloat16)

    def both(pair):
        ahead = [left_table(t) for t in pair] + [right_table(t.T) for t in pair]
        back = [left_table(t.T) for t in pair] + [right_table(t) for t in pair]
        return ahead, back

    spread_ahead, spread_back = both(spread)
    fourier_ahead, fourier_back = both(fourier)
    return spread_ahead, spread_back, fourier_ahead, fourier_back, np.concatenate([shuffle] * 3, axis=0)


def split(value):
    high = value.astype(jnp.bfloat16)
    low = (value - high.astype(jnp.float32)).astype(jnp.bfloat16)
    return high, low


def left_product(table, value):
    high, low = split(value)
    return jnp.dot(table[...], jnp.concatenate([high, high, low], axis=0), preferred_element_type=jnp.float32)


def right_product(value, table):
    high, low = split(value)
    return jnp.dot(jnp.concatenate([high, high, low], axis=1), table[...], preferred_element_type=jnp.float32)


def halves(value, axis):
    half = value.shape[axis] // 2
    first = lax.slice_in_dim(value, 0, half, axis=axis)
    second = lax.slice_in_dim(value, half, 2 * half, axis=axis)
    return first, second


def apart(real, imag, axis):
    real_a, real_b = halves(real, axis)
    imag_a, imag_b = halves(imag, axis)
    plus = jnp.concatenate([real_a + real_b, imag_a + imag_b], axis=axis)
    minus = jnp.concatenate([real_a - real_b, imag_a - imag_b], axis=axis)
    return plus, minus


def together(plus, minus, axis):
    plus_re, plus_im = halves(plus, axis)
    minus_re, minus_im = halves(minus, axis)
    real = jnp.concatenate([plus_re + minus_re, plus_re - minus_re], axis=axis)
    imag = jnp.concatenate([plus_im + minus_im, plus_im - minus_im], axis=axis)
    return real, imag


def regroup(even, odd, axis):
    even_re, even_im = halves(even, axis)
    odd_re, odd_im = halves(odd, axis)
    return jnp.concatenate([even_re, odd_re], axis=axis), jnp.concatenate([even_im, odd_im], axis=axis)


def spread(real, imag, tables):
    left_even, left_odd, right_even, right_odd = tables
    plus, minus = apart(real, imag, 0)
    real, imag = together(left_product(left_even, plus), left_product(left_odd, minus), 0)
    plus, minus = apart(real, imag, 1)
    return together(right_product(plus, right_even), right_product(minus, right_odd), 1)


def to_frequencies(real, imag, tables):
    left_even, left_odd, right_even, right_odd = tables
    plus, minus = apart(real, imag, 0)
    real, imag = regroup(left_product(left_even, plus), left_product(left_odd, minus), 0)
    plus, minus = apart(real, imag, 1)
    return regroup(right_product(plus, right_even), right_product(minus, right_odd), 1)


def from_frequencies(real, imag, tables):
    left_even, left_odd, right_even, right_odd = tables
    even, odd = regroup(real, imag, 0)
    real, imag = together(left_product(left_even, even), left_product(left_odd, odd), 0)
    even, odd = regroup(real, imag, 1)
    return together(right_product(even, right_even), right_product(odd, right_odd), 1)


def place_of(offsets, slot, points):
    row, column = offsets[2 * slot], offsets[2 * slot + 1]
    top = pl.multiple_of(row // 8 * 8, 8)
    start = pl.multiple_of(column // 128 * 128, 128)
    return pl.ds(top, points + 8), pl.ds(start, points + 128), row - top, column - start


def window_of(canvas, offsets, slot, points):
    rows, columns, down, along = place_of(offsets, slot, points)
    parts = []
    for part in range(2):
        wide = canvas[part, rows, columns]
        wide = pltpu.roll(wide, lax.rem(points + 128 - along, points + 128), 1)[:, :points]
        parts.append(pltpu.roll(wide, lax.rem(points + 8 - down, points + 8), 0)[:points])
    return parts


def add_window(canvas, offsets, slot, points, parts):
    rows, columns, down, along = place_of(offsets, slot, points)
    for part in range(2):
        wide = jnp.concatenate([parts[part], jnp.zeros((8, points), jnp.float32)], axis=0)
        wide = pltpu.roll(wide, down, 0)
        wide = jnp.concatenate([wide, jnp.zeros((points + 8, 128), jnp.float32)], axis=1)
        canvas[part, rows, columns] += pltpu.roll(wide, along, 1)


def gather_canvas(layer, tile, right, lower, corner, canvas, sems):
    rows, cols = tile.shape[2], tile.shape[3]
    points = right.shape[2]
    copies = [
        pltpu.make_async_copy(tile.at[layer], canvas.at[:, pl.ds(0, rows), pl.ds(0, cols)], sems.at[0]),
        pltpu.make_async_copy(right, canvas.at[:, pl.ds(0, rows), pl.ds(cols, points)], sems.at[1]),
        pltpu.make_async_copy(lower, canvas.at[:, pl.ds(rows, points), pl.ds(0, cols)], sems.at[2]),
        pltpu.make_async_copy(corner, canvas.at[:, pl.ds(rows, points), pl.ds(cols, points)], sems.at[3]),
    ]
    for copy in copies:
        copy.start()
    for copy in copies:
        copy.wait()


def spread_out_canvas(canvas, tile, right, lower, sems):
    rows, cols = tile.shape[1], tile.shape[2]
    points = lower.shape[1]
    copies = [
        pltpu.make_async_copy(canvas.at[:, pl.ds(0, rows), pl.ds(0, cols)], tile, sems.at[0]),
        pltpu.make_async_copy(canvas.at[:, :, pl.ds(cols, points)], right, sems.at[1]),
        pltpu.make_async_copy(canvas.at[:, pl.ds(rows, points), pl.ds(0, cols)], lower, sems.at[2]),
    ]
    for copy in copies:
        copy.start()
    for copy in copies:
        copy.wait()


def first_kernel(offsets, count, owners, tile, right, lower, corner, probe, t0, t1, t2, t3, wave, canvas, sems):
    slot = pl.program_id(0)

    @pl.when(slot == 0)
    def _():
        gather_canvas(0, tile, right, lower, corner, canvas, sems)

    @pl.when(slot < count[0])
    def _():
        points = probe.shape[1]
        win_re, win_im = window_of(canvas, offsets, slot, points)
        probe_re, probe_im = probe[0], probe[1]
        real = probe_re * win_re - probe_im * win_im
        imag = probe_re * win_im + probe_im * win_re
        real, imag = spread(real, imag, (t0, t1, t2, t3))
        wave[0, 0] = real
        wave[0, 1] = imag


def second_kernel(offsets, count, owners, tile, right, lower, corner, wave, frame, a0, a1, a2, a3, b0, b1, b2, b3, shuffle, grad_wave,
                  grad_tile, grad_right, grad_lower, canvas, grad, sems, columns):
    slot = pl.program_id(0)

    @pl.when(slot == 0)
    def _():
        grad[...] = jnp.zeros_like(grad)
        gather_canvas(1, tile, right, lower, corner, canvas, sems)

    @pl.when(slot < count[0])
    def _():
        points = wave.shape[2]
        half = points // 2
        win_re, win_im = window_of(canvas, offsets, slot, points)
        wave_re, wave_im = wave[0, 0], wave[0, 1]
        real = wave_re * win_re - wave_im * win_im
        imag = wave_re * win_im + wave_im * win_re
        real, imag = to_frequencies(real, imag, (a0, a1, a2, a3))
        pieces = []
        for side in range(points // 128):
            columns[side] = jnp.sqrt(frame[0, :, pl.ds(side * 128, 128)] + BACKGROUND)
            pieces.append(jnp.concatenate([columns[side, pl.ds(start, half, stride=2), :] for start in range(2)], axis=0))
        target = jnp.concatenate(pieces, axis=1)
        high = target.astype(jnp.bfloat16)
        rest = target - high.astype(jnp.float32)
        middle = rest.astype(jnp.bfloat16)
        low = (rest - middle.astype(jnp.float32)).astype(jnp.bfloat16)
        target = jnp.dot(jnp.concatenate([high, middle, low], axis=1), shuffle[...], preferred_element_type=jnp.float32)
        pull = 2.0 - 2.0 * target * lax.rsqrt(real * real + imag * imag + BACKGROUND)
        real, imag = from_frequencies(pull * real, pull * imag, (b0, b1, b2, b3))
        win_re, win_im = window_of(canvas, offsets, slot, points)
        wave_re, wave_im = wave[0, 0], wave[0, 1]
        grad_wave[0, 0] = win_re * real + win_im * imag
        grad_wave[0, 1] = win_re * imag - win_im * real
        add_window(grad, offsets, slot, points, [wave_re * real + wave_im * imag, wave_re * imag - wave_im * real])

    @pl.when(slot == pl.num_programs(0) - 1)
    def _():
        spread_out_canvas(grad, grad_tile, grad_right, grad_lower, sems)


def third_kernel(offsets, count, owners, tile, right, lower, corner, probe, grad_wave, b0, b1, b2, b3, grad_probe, grad_tile,
                 grad_right, grad_lower, canvas, grad, sems):
    slot = pl.program_id(0)

    @pl.when(slot == 0)
    def _():
        grad[...] = jnp.zeros_like(grad)
        grad_probe[...] = jnp.zeros_like(grad_probe)
        gather_canvas(0, tile, right, lower, corner, canvas, sems)

    @pl.when(slot < count[0])
    def _():
        points = probe.shape[1]
        real, imag = spread(grad_wave[0, 0], grad_wave[0, 1], (b0, b1, b2, b3))
        win_re, win_im = window_of(canvas, offsets, slot, points)
        probe_re, probe_im = probe[0], probe[1]
        grad_probe[0] += win_re * real + win_im * imag
        grad_probe[1] += win_re * imag - win_im * real
        add_window(grad, offsets, slot, points, [probe_re * real + probe_im * imag, probe_re * imag - probe_im * real])

    @pl.when(slot == pl.num_programs(0) - 1)
    def _():
        spread_out_canvas(grad, grad_tile, grad_right, grad_lower, sems)


def whole(array):
    return pl.BlockSpec(array.shape, lambda *_: (0,) * array.ndim)


ANY = pl.BlockSpec(memory_space=pl.ANY)


def per_slot(points):
    return pl.BlockSpec((1, 2, points, points), lambda slot, offsets, count, owners: (jnp.minimum(slot, count[0] - 1), 0, 0, 0))


def call(kernel, scalars, operands, in_specs, out_shapes, out_specs, scratch, flops):
    return pl.pallas_call(
        kernel,
        out_shape=out_shapes,
        grid_spec=pltpu.PrefetchScalarGridSpec(
            num_scalar_prefetch=len(scalars),
            grid=(TILE_CAP,),
            in_specs=in_specs,
            out_specs=out_specs,
            scratch_shapes=scratch,
        ),
        compiler_params=pltpu.CompilerParams(vmem_limit_bytes=VMEM_LIMIT),
        cost_estimate=pl.CostEstimate(flops=flops, bytes_accessed=16 * 1024 * 1024, transcendentals=0),
    )(*scalars, *operands)


def probe_kernel(grad, probe, out, from_row, row_sum, from_column, send_sems, recv_sems):
    down, along = lax.axis_index("ty"), lax.axis_index("tx")
    n_down, n_along = lax.axis_size("ty"), lax.axis_size("tx")
    part = grad.shape[0] // n_along
    piece = part // n_down
    barrier = pltpu.get_barrier_semaphore()
    row_peers = [(down, lax.rem(along + step, n_along)) for step in range(1, n_along)]
    column_peers = [(lax.rem(down + step, n_down), along) for step in range(1, n_down)]
    for peer in row_peers + column_peers:
        pl.semaphore_signal(barrier, inc=1, device_id=peer, device_id_type=MESH)
    pl.semaphore_wait(barrier, n_along + n_down - 2)

    def exchange(index, source, target, peer):
        copy = pltpu.make_async_remote_copy(
            src_ref=source, dst_ref=target, send_sem=send_sems.at[index], recv_sem=recv_sems.at[index],
            device_id=peer, device_id_type=MESH)
        copy.start()
        return copy

    def rows(start, size):
        return pl.ds(pl.multiple_of(start, 8), size)

    copies = [
        exchange(step, grad.at[rows(peer[1] * part, part)], from_row.at[step], peer)
        for step, peer in enumerate(row_peers)
    ]
    total = grad[rows(along * part, part)]
    for step, copy in enumerate(copies):
        copy.wait()
        total = total + from_row[step]
    row_sum[...] = total
    base = len(row_peers)
    copies = [
        exchange(base + step, row_sum.at[rows(peer[0] * piece, piece)], from_column.at[step], peer)
        for step, peer in enumerate(column_peers)
    ]
    total = row_sum[rows(down * piece, piece)]
    for step, copy in enumerate(copies):
        copy.wait()
        total = total + from_column[step]
    mine = rows(along * part + down * piece, piece)
    out[mine] = probe[mine] - total
    base += len(column_peers)
    copies = [exchange(base + step, out.at[mine], out.at[mine], peer) for step, peer in enumerate(column_peers)]
    for copy in copies:
        copy.wait()
    base += len(column_peers)
    mine = rows(along * part, part)
    copies = [exchange(base + step, out.at[mine], out.at[mine], peer) for step, peer in enumerate(row_peers)]
    for copy in copies:
        copy.wait()


def update_probe(grad_probe, probe_wave, scale):
    shape = probe_wave.shape
    flat = (probe_wave.size // 128, 128)
    n_down, n_along = lax.axis_size("ty"), lax.axis_size("tx")
    part = flat[0] // n_along
    piece = part // n_down
    copies = 2 * (n_along + n_down - 2)
    vmem = pl.BlockSpec(memory_space=pltpu.VMEM)
    out = pl.pallas_call(
        probe_kernel,
        out_shape=jax.ShapeDtypeStruct(flat, jnp.float32),
        in_specs=[vmem, vmem],
        out_specs=vmem,
        scratch_shapes=[
            pltpu.VMEM((n_along - 1, part, 128), jnp.float32),
            pltpu.VMEM((part, 128), jnp.float32),
            pltpu.VMEM((n_down - 1, piece, 128), jnp.float32),
            pltpu.SemaphoreType.DMA((copies,)),
            pltpu.SemaphoreType.DMA((copies,)),
        ],
        compiler_params=pltpu.CompilerParams(collective_id=1, has_side_effects=True),
    )((grad_probe * scale).reshape(flat), probe_wave.reshape(flat))
    return out.reshape(shape)


def local(object_slab, probe_wave, frames, scan_tiles, scan_offsets):
    columns = lax.axis_size("tx")
    row_index = lax.axis_index("ty")
    col_index = lax.axis_index("tx")
    owned = frames.shape[0]
    points = probe_wave.shape[-1]
    layers, _, tile_rows, tile_cols = object_slab.shape
    total_frames = owned * columns
    my_tile = row_index * columns + col_index
    by_owner = scan_tiles.reshape(columns, owned)

    mine = lax.dynamic_index_in_dim(by_owner, col_index, 0, keepdims=False)
    wanted = row_index * columns + jnp.arange(columns, dtype=jnp.int32)
    source = jnp.sum((mine[None, :] == wanted[:, None]).astype(jnp.int32) * jnp.arange(owned, dtype=jnp.int32)[None, :], axis=1)

    def pick_kernel(source_ref, frames_ref, out_ref, sems):
        copies = [
            pltpu.make_async_copy(frames_ref.at[source_ref[place]], out_ref.at[place], sems.at[place])
            for place in range(columns)
        ]
        for copy in copies:
            copy.start()
        for copy in copies:
            copy.wait()

    outgoing = pl.pallas_call(
        pick_kernel,
        out_shape=jax.ShapeDtypeStruct((columns, points, points), jnp.float32),
        grid_spec=pltpu.PrefetchScalarGridSpec(
            num_scalar_prefetch=1, grid=(1,), in_specs=[ANY], out_specs=ANY,
            scratch_shapes=[pltpu.SemaphoreType.DMA((columns,))]),
        cost_estimate=pl.CostEstimate(flops=0, bytes_accessed=8 * 1024 * 1024, transcendentals=0),
    )(source, frames)
    arrived = lax.all_to_all(outgoing, "tx", split_axis=0, concat_axis=0, tiled=True)

    matches = by_owner == my_tile
    present = jnp.any(matches, axis=1)
    which = jnp.sum(matches.astype(jnp.int32) * jnp.arange(owned, dtype=jnp.int32)[None, :], axis=1)
    global_ids = jnp.arange(columns, dtype=jnp.int32) * owned + which
    ranks = jnp.cumsum(present.astype(jnp.int32)) - 1
    slot_pick = (present[None, :] & (ranks[None, :] == jnp.arange(TILE_CAP, dtype=jnp.int32)[:, None])).astype(jnp.int32)
    chosen_ids = jnp.sum(slot_pick * global_ids[None, :], axis=1)
    owners = jnp.sum(slot_pick * jnp.arange(columns, dtype=jnp.int32)[None, :], axis=1)
    count = jnp.sum(present.astype(jnp.int32)).reshape(1)
    offsets = scan_offsets[chosen_ids].reshape(-1)
    scalars = (offsets, count, owners)

    halos = []
    for layer in range(layers):
        right = passed_along(object_slab[layer, :, :, :points], "tx", -1)
        lower = passed_along(object_slab[layer, :, :points, :], "ty", -1)
        corner = passed_along(lower[:, :, :points], "tx", -1)
        halos.append((right, lower, corner))

    spread_ahead, spread_back, fourier_ahead, fourier_back, shuffle = build_tables(points)
    slot_spec = pl.BlockSpec((1, 2, points, points), lambda slot, offsets, count, owners: (slot, 0, 0, 0))
    frame_spec = pl.BlockSpec((1, points, points), lambda slot, offsets, count, owners: (owners[slot], 0, 0))
    waves = jax.ShapeDtypeStruct((TILE_CAP, 2, points, points), jnp.float32)
    canvas = pltpu.VMEM((2, tile_rows + points, tile_cols + points), jnp.float32)
    sems = pltpu.SemaphoreType.DMA((4,))
    flops = TILE_CAP * 24 * points**3
    grads = [
        jax.ShapeDtypeStruct((2, tile_rows, tile_cols), jnp.float32),
        jax.ShapeDtypeStruct((2, tile_rows + points, points), jnp.float32),
        jax.ShapeDtypeStruct((2, points, tile_cols), jnp.float32),
    ]

    wave = call(
        first_kernel, scalars, (object_slab, *halos[0], probe_wave, *spread_ahead),
        [ANY] * 4 + [whole(probe_wave)] + [whole(t) for t in spread_ahead],
        waves, slot_spec, [canvas, sems], flops)
    grad_wave, *grad_one = call(
        second_kernel, scalars, (object_slab, *halos[1], wave, arrived, *fourier_ahead, *fourier_back, shuffle),
        [ANY] * 4 + [slot_spec, frame_spec] + [whole(t) for t in (*fourier_ahead, *fourier_back, shuffle)],
        [waves] + grads, [slot_spec] + [ANY] * 3, [canvas, canvas, sems, pltpu.VMEM((points // 128, points, 128), jnp.float32)], 2 * flops)
    grad_probe, *grad_zero = call(
        third_kernel, scalars, (object_slab, *halos[0], probe_wave, grad_wave, *spread_back),
        [ANY] * 4 + [whole(probe_wave), slot_spec] + [whole(t) for t in spread_back],
        [jax.ShapeDtypeStruct(probe_wave.shape, jnp.float32)] + grads,
        [whole(probe_wave)] + [ANY] * 3, [canvas, canvas, sems], flops)

    totals = []
    for tile, right, lower in (grad_zero, grad_one):
        right_back = passed_along(right, "tx", 1)
        lower = lower.at[:, :, :points].add(right_back[:, tile_rows:])
        lower_back = passed_along(lower, "ty", 1)
        tile = tile.at[:, :, :points].add(right_back[:, :tile_rows])
        totals.append(tile.at[:, :points, :].add(lower_back))
    new_probe = update_probe(grad_probe, probe_wave, PROBE_RATE / total_frames)
    return (object_slab - OBJECT_RATE * jnp.stack(totals), new_probe)


def solution(mesh):
    return jax.shard_map(
        local,
        mesh=mesh,
        in_specs=(P(None, None, "ty", "tx"), P(), P("tx", None, None), P(), P()),
        out_specs=(P(None, None, "ty", "tx"), P()),
        check_vma=False,
    )
```

time: 752 us -> 417 us (0.55)
  the two profiles are of different devices: /device:TPU:1 before, /device:TPU:104 now
where the time goes in v1:
time: 417 us; the launch traced here: 412 us
  Pallas kernels  248 us (59%)
  waiting for transfers between devices  88.7 us (21%)
  starting transfers between devices  40.7 us (10%)
  other arithmetic  16.5 us (4%)
  local copies, waits for them, and re-layouts  16.2 us (4%)
    pallas_call x1, Pallas kernels, local(): pl.pallas_call(pick_kernel, out_shape=jax.ShapeDtypeStruct((columns, poin...  129 us
    ppermute x10, waiting for transfers between devices, passed_along(): lax.ppermute(value, axis, [(source, source + steps) for source in range(l...  88.7 us
    pallas_call x3, Pallas kernels, call(): pl.pallas_call(kernel, out_shape=out_shapes, grid_spec=pltpu.PrefetchScal...  65.5 us
    pallas_call x1, Pallas kernels, update_probe(): pl.pallas_call(probe_kernel, out_shape=jax.ShapeDtypeStruct(flat, jnp.flo...  54 us
    ppermute x10, starting transfers between devices, passed_along(): lax.ppermute(value, axis, [(source, source + steps) for source in range(l...  34.9 us
  transfers between devices with their start and end apart: 11, of which 4 were waited for; matrix products, arithmetic and copies ran while one was open for 6% of the time, Pallas kernels for 17%

profile of v1, /device:TPU:104, one launch (start us, length us, event | category | flops | bytes accessed | tf_op | source)
XLA Modules:
  0.0 411.6 jit_solution(10313343275389556913)
XLA Ops:
  2.1 129.0 %shard_map.222 = f32[16,256,256]{2,1,0:T(8,128)} custom-call(s32[16]{0:T(128)} %select_reduce_fusion.source_ref, f32[48,256,256]{2,1,0:T(8,128)} %frames_ref.1), custom_call_target="tpu_custom_call" | custom-call | bytes 8388608 | tf_op jit(solution)/shard_map/pallas_call | solution.py:417
  131.1 5.8 %all-to-all-start = ((f32[16,256,256]{2,1,0:T(8,128)}), f32[16,256,256]{2,1,0:T(8,128)}, u32[]{:S(2)}, u32[]{:S(2)}) async-start(f32[16,256,256]{2,1,0:T(8,128)} %shard_map.222), calls=%async_computation | async-start | bytes 8388608 | tf_op jit(solution)/shard_map/all_to_all | solution.py:425
  136.9 2.9 slice_bitcast_fusion.2
  139.9 4.8 %collective-permute-start.1 = (f32[2,256,512]{2,1,0:T(8,128)S(1)}, f32[2,256,512]{2,1,0:T(8,128)S(1)}, u32[]{:S(2)}, u32[]{:S(2)}) collective-permute-start(f32[2,256,512]{2,1,0:T(8,128)S(1)} %get-tuple-element.94), channel_id=1, source_target_pairs={{16,0},{32,16},{48,32},{64,48},{80,64},{96,80},{112,96},{17,1},{33... | collective-permute-start | bytes 3145736 | tf_op jit(solution)/shard_map/ppermute | solution.py:25
  144.7 1.6 slice_bitcast_fusion.3
  146.3 1.9 collective-permute-start
  148.2 2.8 collective-permute-start.4
  151.0 1.9 collective-permute-start.3
  155.3 28.4 %collective-permute-done.1.lower = f32[2,256,512]{2,1,0:T(8,128)S(1)} collective-permute-done((f32[2,256,512]{2,1,0:T(8,128)S(1)}, f32[2,256,512]{2,1,0:T(8,128)S(1)}, u32[]{:S(2)}, u32[]{:S(2)}) %collective-permute-start.1) | collective-permute-done | bytes 1048608 | tf_op jit(solution)/shard_map/ppermute | solution.py:25
  183.8 1.9 collective-permute-start.2
  185.7 1.3 select_reduce_fusion.2
  187.0 30.3 %collective-permute-done.4.lower = f32[2,256,512]{2,1,0:T(8,128)} collective-permute-done((f32[2,256,512]{2,1,0:T(8,128)}, f32[2,256,512]{2,1,0:T(8,128)}, u32[]{:S(2)}, u32[]{:S(2)}) %collective-permute-start.4) | collective-permute-done | bytes 1048608 | tf_op jit(solution)/shard_map/ppermute | solution.py:25
  217.4 1.9 slice.193
  219.2 13.8 %collective-permute-start.5 = (f32[2,256,256]{2,1,0:T(8,128)}, f32[2,256,256]{2,1,0:T(8,128)}, u32[]{:S(2)}, u32[]{:S(2)}) collective-permute-start(f32[2,256,256]{2,1,0:T(8,128)} %slice.193), channel_id=1, source_target_pairs={{1,0},{2,1},{3,2},{4,3},{5,4},{6,5},{7,6},{8,7},{9,8},{10,9},{11,1... | collective-permute-start | bytes 1572872 | tf_op jit(solution)/shard_map/ppermute | solution.py:25
  236.0 15.7 %shard_map.221.wave = f32[8,2,256,256]{3,2,1,0:T(8,128)} custom-call(s32[16]{0:T(128)} %reshape.257.offsets, s32[1]{0:T(128)} %bitcast.3.count, s32[8]{0:T(128)} %get-tuple-element.90.owners, f32[2,2,512,512]{3,2,1,0:T(8,128)} %tile.5, f32[2,512,256]{2,1,0:T(8,128)} %copy-done.6, f32[2,256,512]{2,1,0:T(8,128)} %copy-done.4, f32[2,256,256]{2,1,0:T(8,128)} %copy-done.7, ...), custom_call_target="tpu_custom_call" | custom-call | flops 3221225472 | bytes 16777216 | tf_op jit(solution)/shard_map/pallas_call | solution.py:299
  251.8 31.1 %shard_map.223 = (f32[8,2,256,256]{3,2,1,0:T(8,128)}, f32[2,512,512]{2,1,0:T(8,128)}, f32[2,768,256]{2,1,0:T(8,128)}, f32[2,256,512]{2,1,0:T(8,128)}) custom-call(s32[16]{0:T(128)} %reshape.257.offsets, s32[1]{0:T(128)} %bitcast.3.count, s32[8]{0:T(128)} %get-tuple-element.90.owners, f32[2,2,512,512]{3,2,1,0:T(8,128)} %tile.5, ...), custom_call_target="tpu_custom_call" | custom-call | flops 6442450944 | bytes 16777216 | tf_op jit(solution)/shard_map/pallas_call | solution.py:299
  282.8 18.8 %shard_map.224 = (f32[2,256,256]{2,1,0:T(8,128)}, f32[2,512,512]{2,1,0:T(8,128)}, f32[2,768,256]{2,1,0:T(8,128)}, f32[2,256,512]{2,1,0:T(8,128)}) custom-call(s32[16]{0:T(128)} %reshape.257.offsets, s32[1]{0:T(128)} %bitcast.3.count, s32[8]{0:T(128)} %get-tuple-element.90.owners, f32[2,2,512,512]{3,2,1,0:T(8,128)} %tile.5, f32[2,512,256]{2,1,0:T(8,128)} %copy-done.6, ...), custom_call_target="tpu_custom_call" | custom-call | flops 3221225472 | bytes 16777216 | tf_op jit(solution)/shard_map/pallas_call | solution.py:299
  301.6 1.9 collective-permute-start.6
  303.6 2.1 collective-permute-start.8
  306.5 17.2 %collective-permute-done.6 = f32[2,768,256]{2,1,0:T(8,128)} collective-permute-done((f32[2,768,256]{2,1,0:T(8,128)}, f32[2,768,256]{2,1,0:T(8,128)}, u32[]{:S(2)}, u32[]{:S(2)}) %collective-permute-start.6) | collective-permute-done | bytes 1572896 | tf_op jit(solution)/shard_map/ppermute | solution.py:25
  323.7 2.1 fusion.8
  325.8 1.9 collective-permute-start.7
  327.7 12.7 %collective-permute-done.8 = f32[2,768,256]{2,1,0:T(8,128)S(1)} collective-permute-done((f32[2,768,256]{2,1,0:T(8,128)}, f32[2,768,256]{2,1,0:T(8,128)S(1)}, u32[]{:S(2)}, u32[]{:S(2)}) %collective-permute-start.8) | collective-permute-done | bytes 1572896 | tf_op jit(solution)/shard_map/ppermute | solution.py:25
  340.4 2.3 fusion.7
  342.7 1.9 collective-permute-start.9
  345.5 54.0 %shard_map.225 = f32[1024,128]{1,0:T(8,128)} custom-call(f32[1024,128]{1,0:T(8,128)} %reshape.259.grad, f32[1024,128]{1,0:T(8,128)} %reshape.260.probe), custom_call_target="tpu_custom_call" | custom-call | tf_op jit(solution)/shard_map/pallas_call | solution.py:375
  399.5 2.0 reshape.261
  401.5 1.5 fusion.6
  403.2 1.4 copy-done.2
  405.5 1.6 fusion.5
  407.1 1.4 fusion.2
  408.6 3.0 fusion
  (58 shorter events, 9.7 us)
Async XLA Ops:
  131.1 120.7 %all-to-all-start = ((f32[16,256,256]{2,1,0:T(8,128)}), f32[16,256,256]{2,1,0:T(8,128)}, u32[]{:S(2)}, u32[]{:S(2)}) async-start(f32[16,256,256]{2,1,0:T(8,128)} %shard_map.222), calls=%async_computation | async-start | bytes 8388608 | tf_op jit(solution)/shard_map/all_to_all | solution.py:425
  136.9 7.7 %copy-start = (f32[2,2,512,512]{3,2,1,0:T(8,128)S(1)}, f32[2,2,512,512]{3,2,1,0:T(8,128)}, u32[]{:S(2)}) copy-start(f32[2,2,512,512]{3,2,1,0:T(8,128)} %tile.5) | copy-start | bytes 12582916
  139.9 14.5 %copy-start.11 = (s32[768,2]{0,1:T(2,128)S(1)}, s32[768,2]{0,1:T(2,128)}, u32[]{:S(2)}) copy-start(s32[768,2]{0,1:T(2,128)} %param.38) | copy-start | bytes 18436
  139.9 43.9 %collective-permute-start.1 = (f32[2,256,512]{2,1,0:T(8,128)S(1)}, f32[2,256,512]{2,1,0:T(8,128)S(1)}, u32[]{:S(2)}, u32[]{:S(2)}) collective-permute-start(f32[2,256,512]{2,1,0:T(8,128)S(1)} %get-tuple-element.94), channel_id=1, source_target_pairs={{16,0},{32,16},{48,32},{64,48},{80,64},{96,80},{112,96},{17,1},{33... | collective-permute-start | bytes 3145736 | tf_op jit(solution)/shard_map/ppermute | solution.py:25
  146.3 88.6 %collective-permute-start = (f32[2,512,256]{2,1,0:T(8,128)}, f32[2,512,256]{2,1,0:T(8,128)S(1)}, u32[]{:S(2)}, u32[]{:S(2)}) collective-permute-start(f32[2,512,256]{2,1,0:T(8,128)} %get-tuple-element.96), channel_id=1, source_target_pairs={{1,0},{2,1},{3,2},{4,3},{5,4},{6,5},{7,6},{8,7},{9,8},{10,9},{11,1... | collective-permute-start | bytes 3145736 | tf_op jit(solution)/shard_map/ppermute | solution.py:25
  148.2 69.2 %collective-permute-start.4 = (f32[2,256,512]{2,1,0:T(8,128)}, f32[2,256,512]{2,1,0:T(8,128)}, u32[]{:S(2)}, u32[]{:S(2)}) collective-permute-start(f32[2,256,512]{2,1,0:T(8,128)} %get-tuple-element.95), channel_id=1, source_target_pairs={{16,0},{32,16},{48,32},{64,48},{80,64},{96,80},{112,96},{17,1},{33... | collective-permute-start | bytes 3145736 | tf_op jit(solution)/shard_map/ppermute | solution.py:25
  151.0 100.7 %collective-permute-start.3 = (f32[2,512,256]{2,1,0:T(8,128)}, f32[2,512,256]{2,1,0:T(8,128)}, u32[]{:S(2)}, u32[]{:S(2)}) collective-permute-start(f32[2,512,256]{2,1,0:T(8,128)} %get-tuple-element.97), channel_id=1, source_target_pairs={{1,0},{2,1},{3,2},{4,3},{5,4},{6,5},{7,6},{8,7},{9,8},{10,9},{11,1... | collective-permute-start | bytes 3145736 | tf_op jit(solution)/shard_map/ppermute | solution.py:25
  153.7 0.5 copy-start.12
  154.5 79.6 %copy-start.13 = (pred[16]{0:T(512)(128)(4,1)S(1)}, pred[16]{0:T(512)(128)(4,1)}, u32[]{:S(2)}) copy-start(pred[16]{0:T(512)(128)(4,1)} %copy-done.12) | copy-start | bytes 52
  183.7 51.1 %copy-start.4 = (f32[2,256,512]{2,1,0:T(8,128)}, f32[2,256,512]{2,1,0:T(8,128)S(1)}, u32[]{:S(2)}) copy-start(f32[2,256,512]{2,1,0:T(8,128)S(1)} %collective-permute-done.1.lower) | copy-start | bytes 3145732
  183.8 51.1 %collective-permute-start.2 = (f32[2,256,256]{2,1,0:T(8,128)S(1)}, f32[2,256,256]{2,1,0:T(8,128)S(1)}, u32[]{:S(2)}, u32[]{:S(2)}) collective-permute-start(f32[2,256,256]{2,1,0:T(8,128)S(1)} %slice.192), channel_id=1, source_target_pairs={{1,0},{2,1},{3,2},{4,3},{5,4},{6,5},{7,6},{8,7},{9,8},{10,9},{11,1... | collective-permute-start | bytes 1572872 | tf_op jit(solution)/shard_map/ppermute | solution.py:25
  219.2 32.5 %collective-permute-start.5 = (f32[2,256,256]{2,1,0:T(8,128)}, f32[2,256,256]{2,1,0:T(8,128)}, u32[]{:S(2)}, u32[]{:S(2)}) collective-permute-start(f32[2,256,256]{2,1,0:T(8,128)} %slice.193), channel_id=1, source_target_pairs={{1,0},{2,1},{3,2},{4,3},{5,4},{6,5},{7,6},{8,7},{9,8},{10,9},{11,1... | collective-permute-start | bytes 1572872 | tf_op jit(solution)/shard_map/ppermute | solution.py:25
  234.9 1.0 copy-start.6
  234.9 1.1 copy-start.7
  282.8 22.8 %copy-start.5 = (f32[2,256,256]{2,1,0:T(8,128)S(1)}, f32[2,256,256]{2,1,0:T(8,128)}, u32[]{:S(2)}) copy-start(f32[2,256,256]{2,1,0:T(8,128)} %probe.3) | copy-start | bytes 1572868
  301.6 22.1 %collective-permute-start.6 = (f32[2,768,256]{2,1,0:T(8,128)}, f32[2,768,256]{2,1,0:T(8,128)}, u32[]{:S(2)}, u32[]{:S(2)}) collective-permute-start(f32[2,768,256]{2,1,0:T(8,128)} %get-tuple-element.84), channel_id=1, source_target_pairs={{0,1},{1,2},{2,3},{3,4},{4,5},{5,6},{6,7},{7,8},{8,9},{9,10},{10,1... | collective-permute-start | bytes 4718600 | tf_op jit(solution)/shard_map/ppermute | solution.py:25
  303.5 41.1 %copy-start.10 = (f32[2,256,256]{2,1,0:T(8,128)S(1)}, f32[2,256,256]{2,1,0:T(8,128)}, u32[]{:S(2)}) copy-start(f32[2,256,256]{2,1,0:T(8,128)} %get-tuple-element.89) | copy-start | bytes 1572868
  303.6 36.9 %collective-permute-start.8 = (f32[2,768,256]{2,1,0:T(8,128)}, f32[2,768,256]{2,1,0:T(8,128)S(1)}, u32[]{:S(2)}, u32[]{:S(2)}) collective-permute-start(f32[2,768,256]{2,1,0:T(8,128)} %get-tuple-element.87), channel_id=1, source_target_pairs={{0,1},{1,2},{2,3},{3,4},{4,5},{5,6},{6,7},{7,8},{8,9},{9,10},{10,1... | collective-permute-start | bytes 4718600 | tf_op jit(solution)/shard_map/ppermute | solution.py:25
  325.8 79.7 %collective-permute-start.7 = (f32[2,256,512]{2,1,0:T(8,128)}, f32[2,256,512]{2,1,0:T(8,128)}, u32[]{:S(2)}, u32[]{:S(2)}) collective-permute-start(f32[2,256,512]{2,1,0:T(8,128)} %fusion.8), channel_id=1, source_target_pairs={{0,16},{16,32},{32,48},{48,64},{64,80},{80,96},{96,112},{1,17},{17... | collective-permute-start | bytes 3145736 | tf_op jit(solution)/shard_map/ppermute | solution.py:25
  340.4 4.2 %copy-start.8 = (f32[2,768,256]{2,1,0:T(8,128)}, f32[2,768,256]{2,1,0:T(8,128)S(1)}, u32[]{:S(2)}) copy-start(f32[2,768,256]{2,1,0:T(8,128)S(1)} %collective-permute-done.8) | copy-start | bytes 4718596
  342.7 64.4 %collective-permute-start.9 = (f32[2,256,512]{2,1,0:T(8,128)}, f32[2,256,512]{2,1,0:T(8,128)}, u32[]{:S(2)}, u32[]{:S(2)}) collective-permute-start(f32[2,256,512]{2,1,0:T(8,128)} %fusion.7), channel_id=1, source_target_pairs={{0,16},{16,32},{32,48},{48,64},{64,80},{80,96},{96,112},{1,17},{17... | collective-permute-start | bytes 3145736 | tf_op jit(solution)/shard_map/ppermute | solution.py:25
  344.7 56.8 %copy-start.3 = (f32[2,512,512]{2,1,0:T(8,128)S(1)}, f32[2,512,512]{2,1,0:T(8,128)}, u32[]{:S(2)}) copy-start(f32[2,512,512]{2,1,0:T(8,128)} %get-tuple-element.83) | copy-start | bytes 6291460
  403.0 1.6 copy-start.2
  403.0 2.0 copy-start.9
  405.5 3.1 copy-start.1

commit v2 on v1

--- a/solution.py
+++ b/solution.py
@@ -19,10 +19,8 @@
 VMEM_LIMIT = 56 * 1024 * 1024
 
 
-def passed_along(value, axis, steps):
-    count = lax.axis_size(axis)
-    leading, last = (max(0, -steps), min(count, count - steps))
-    return lax.ppermute(value, axis, [(source, source + steps) for source in range(leading, last)])
+FRAME_STEPS = ((1, 0, 0), (3, 0, 0), (0, 1, 1), (2, 0, 0), (1, 1, 1), (3, 1, 1), (0, 1, 0), (2, 1, 1), (1, 0, 1), (3, 0, 1), (2, 0, 1),
+               (1, 1, 0), (3, 1, 0), (2, 1, 0), (0, 0, 1))
 
 
 def real_form(matrix):
@@ -172,17 +170,25 @@
 
 def gather_canvas(layer, tile, right, lower, corner, canvas, sems):
     rows, cols = tile.shape[2], tile.shape[3]
-    points = right.shape[2]
+    points = right.shape[3]
     copies = [
         pltpu.make_async_copy(tile.at[layer], canvas.at[:, pl.ds(0, rows), pl.ds(0, cols)], sems.at[0]),
-        pltpu.make_async_copy(right, canvas.at[:, pl.ds(0, rows), pl.ds(cols, points)], sems.at[1]),
-        pltpu.make_async_copy(lower, canvas.at[:, pl.ds(rows, points), pl.ds(0, cols)], sems.at[2]),
-        pltpu.make_async_copy(corner, canvas.at[:, pl.ds(rows, points), pl.ds(cols, points)], sems.at[3]),
+        pltpu.make_async_copy(right.at[layer], canvas.at[:, pl.ds(0, rows), pl.ds(cols, points)], sems.at[1]),
+        pltpu.make_async_copy(lower.at[layer], canvas.at[:, pl.ds(rows, points), pl.ds(0, cols)], sems.at[2]),
+        pltpu.make_async_copy(corner.at[layer], canvas.at[:, pl.ds(rows, points), pl.ds(cols, points)], sems.at[3]),
     ]
     for copy in copies:
         copy.start()
     for copy in copies:
         copy.wait()
+
+    @pl.when(lax.axis_index("ty") == lax.axis_size("ty") - 1)
+    def _():
+        canvas[:, pl.ds(rows, points), :] = jnp.zeros((2, points, cols + points), jnp.float32)
+
+    @pl.when(lax.axis_index("tx") == lax.axis_size("tx") - 1)
+    def _():
+        canvas[:, :, pl.ds(cols, points)] = jnp.zeros((2, rows + points, points), jnp.float32)
 
 
 def spread_out_canvas(canvas, tile, right, lower, sems):
@@ -311,82 +317,296 @@
     )(*scalars, *operands)
 
 
-def probe_kernel(grad, probe, out, from_row, row_sum, from_column, send_sems, recv_sems):
+def remote(source, target, send_sem, recv_sem, peer):
+    return pltpu.make_async_remote_copy(
+        src_ref=source, dst_ref=target, send_sem=send_sem, recv_sem=recv_sem, device_id=peer, device_id_type=MESH)
+
+
+def when(condition, action):
+    pl.when(condition)(lambda: action())
+
+
+def greet(peers):
+    barrier = pltpu.get_barrier_semaphore()
+    for peer in peers:
+        pl.semaphore_signal(barrier, inc=1, device_id=peer, device_id_type=MESH)
+    pl.semaphore_wait(barrier, len(peers))
+
+
+def around(down, along, n_down, n_along):
+    row = [(down, lax.rem(along + step, n_along)) for step in range(1, n_along)]
+    column = [(lax.rem(down + step, n_down), along) for step in range(1, n_down)]
+    return row, column
+
+
+def frame_peer(down, along, n_down, n_along, step, ahead):
+    step_y, step_z, step_core = step
+    if not ahead:
+        step_y = -step_y % (n_along // 4)
+    place_y, place_z, core = along // 4, lax.rem(along // 2, 2), lax.rem(along, 2)
+    other = step_z * jnp.maximum(step_core, core)
+    place_y = lax.rem(place_y + step_y, n_along // 4)
+    place_z = lax.rem(place_z + step_z, 2)
+    core = lax.rem(core + step_core, 2)
+    return (lax.rem(down + other * (n_down // 2), n_down), place_y * 4 + place_z * 2 + core), other
+
+
+def fetch_kernel(source, frames, slab, right, lower, corner, arrived, held, picked, lower_relay, right_relay, held_sem, own_sem,
+                 send_sems, recv_sems):
     down, along = lax.axis_index("ty"), lax.axis_index("tx")
     n_down, n_along = lax.axis_size("ty"), lax.axis_size("tx")
-    part = grad.shape[0] // n_along
+    layers, points, rows, cols = right.shape[0], right.shape[3], right.shape[2], lower.shape[3]
+    half = n_down // 2
+    load = pltpu.make_async_copy(frames, held, held_sem)
+    load.start()
+    ring = lambda by_down, by_along: (lax.rem(down + by_down + n_down, n_down), lax.rem(along + by_along + n_along, n_along))
+    greet([frame_peer(down, along, n_down, n_along, step, False)[0] for step in FRAME_STEPS]
+          + [ring(by, 0) for by in (1, -1, half, 3, -3)] + [ring(0, by) for by in (1, -1, 3, -3, 4, -4)])
+    above, left = ring(-1, 0), ring(0, -1)
+    not_top, not_bottom = down > 0, down < n_down - 1
+    not_first, not_last = along > 0, along < n_along - 1
+    wraps, passes = down == half, down == 0
+    crosses, carries = lax.rem(along, 4) == 0, lax.rem(along, 4) == 3
+    crossed = carries & not_last
+    across = crosses & not_first
+    base = n_along - 1
+    index = iter(range(base, base + 20))
+
+    def copy(source_ref, target, peer, at=None):
+        at = next(index) if at is None else at
+        return remote(source_ref, target, send_sems.at[at], recv_sems.at[at], peer)
+
+    first, last = 0, layers - 1
+    side = [slab.at[layer, :, :, pl.ds(0, points)] for layer in range(layers)]
+    edge = [lower.at[layer, :, :, pl.ds(0, points)] for layer in range(layers)]
+    rest, start = pl.ds(points, cols - points), pl.ds(0, points)
+    lowers, others, hops, forwards, rights, corners = [], [], [], [], [], []
+    for layer in range(layers):
+        lowers.append(copy(slab.at[layer, :, pl.ds(0, points), start], lower.at[layer, :, :, start], above))
+        at = next(index)
+        others.append(copy(slab.at[layer, :, pl.ds(0, points), rest], lower.at[layer, :, :, rest], above, at))
+        hops.append(copy(slab.at[layer, :, pl.ds(0, points), rest], lower_relay.at[layer], ring(half, 0)))
+        forwards.append(copy(lower_relay.at[layer], lower.at[layer, :, :, rest], ring(3, 0), at))
+        rights.append(copy(side[layer], right.at[layer], left))
+        corners.append(copy(edge[layer], corner.at[layer], left))
+    at_right, at_corner = base + 5 * last + 3, base + 5 * last + 4
+    right_hop = copy(side[last], right_relay.at[:, pl.ds(0, rows), :], ring(0, 3))
+    right_forward = copy(right_relay.at[:, pl.ds(0, rows), :], right.at[last], ring(0, -4), at_right)
+    corner_hop = copy(edge[last], right_relay.at[:, pl.ds(rows, points), :], ring(0, 3))
+    corner_forward = copy(right_relay.at[:, pl.ds(rows, points), :], corner.at[last], ring(0, -4), at_corner)
+
+    for layer in range(layers):
+        when(not_top, lowers[layer].start)
+        when(not_top & ~wraps, others[layer].start)
+        when(wraps, hops[layer].start)
+    when(across, right_hop.start)
+    when(not_first & ~crosses, rights[last].start)
+    when(not_first, rights[first].start)
+    load.wait()
+    sends = []
+    for step, offset in enumerate(FRAME_STEPS):
+        peer, other = frame_peer(down, along, n_down, n_along, offset, True)
+        picked[step] = held[source[other * n_along + peer[1]]]
+        send = remote(picked.at[step], arrived.at[along], send_sems.at[step], recv_sems.at[step], peer)
+        send.start()
+        sends.append(send)
+    picked[n_along - 1] = held[source[along]]
+    own = pltpu.make_async_copy(picked.at[n_along - 1], arrived.at[along], own_sem)
+    own.start()
+    relays = along >= 4
+    when(carries & relays, right_hop.wait_recv)
+    when(carries & relays, right_forward.start)
+    for layer in range(layers):
+        when(passes, hops[layer].wait_recv)
+        when(passes, forwards[layer].start)
+        when(not_bottom, lowers[layer].wait_recv)
+        if layer == last:
+            when(not_bottom & across, corner_hop.start)
+            when(not_bottom & not_first & ~crosses, corners[layer].start)
+            when(not_bottom & carries & relays, corner_hop.wait_recv)
+            when(not_bottom & carries & relays, corner_forward.start)
+        else:
+            when(not_bottom & not_first, corners[layer].start)
+    for layer in range(layers):
+        when(not_bottom, others[layer].wait_recv)
+        when(not_last, rights[layer].wait_recv)
+        when(not_bottom & not_last, corners[layer].wait_recv)
+        when(not_top, lowers[layer].wait_send)
+        when(not_top & ~wraps, others[layer].wait_send)
+        when(wraps, hops[layer].wait_send)
+        when(passes, forwards[layer].wait_send)
+        if layer == last:
+            when(across, right_hop.wait_send)
+            when(not_first & ~crosses, rights[layer].wait_send)
+            when(carries & relays, right_forward.wait_send)
+            when(not_bottom & across, corner_hop.wait_send)
+            when(not_bottom & not_first & ~crosses, corners[layer].wait_send)
+            when(not_bottom & carries & relays, corner_forward.wait_send)
+        else:
+            when(not_first, rights[layer].wait_send)
+            when(not_bottom & not_first, corners[layer].wait_send)
+    for send in sends:
+        send.wait()
+    own.wait()
+
+
+def fetch(source, frames, object_slab, points):
+    layers, _, rows, cols = object_slab.shape
+    n_along = lax.axis_size("tx")
+    copies = n_along - 1 + 5 * layers + 2
+    shape = lambda *dims: jax.ShapeDtypeStruct(dims, jnp.float32)
+    return pl.pallas_call(
+        fetch_kernel,
+        out_shape=[shape(layers, 2, rows, points), shape(layers, 2, points, cols), shape(layers, 2, points, points),
+                   shape(n_along, points, points)],
+        in_specs=[pl.BlockSpec(memory_space=pltpu.SMEM), ANY, ANY],
+        out_specs=[ANY] * 4,
+        scratch_shapes=[
+            pltpu.VMEM(frames.shape, jnp.float32),
+            pltpu.VMEM((n_along, points, points), jnp.float32),
+            pltpu.VMEM((layers, 2, points, cols - points), jnp.float32),
+            pltpu.VMEM((2, rows + points, points), jnp.float32),
+            pltpu.SemaphoreType.DMA,
+            pltpu.SemaphoreType.DMA,
+            pltpu.SemaphoreType.DMA((copies,)),
+            pltpu.SemaphoreType.DMA((copies,)),
+        ],
+        compiler_params=pltpu.CompilerParams(collective_id=0, has_side_effects=True, vmem_limit_bytes=VMEM_LIMIT),
+    )(source, frames, object_slab)
+
+
+def return_kernel(right_0, right_1, lower_0, lower_1, grad_probe, probe, right_in, lower_in, probe_out,
+                  corner_in, held, relay, from_row, row_sum, from_column, load_sems, send_sems, recv_sems):
+    down, along = lax.axis_index("ty"), lax.axis_index("tx")
+    n_down, n_along = lax.axis_size("ty"), lax.axis_size("tx")
+    rights, lowers = (right_0, right_1), (lower_0, lower_1)
+    layers, points, rows, cols = len(rights), right_in.shape[3], right_in.shape[2], lower_in.shape[3]
+    loads = [
+        pltpu.make_async_copy(lowers[layer].at[:, :, pl.ds(0, points)], held.at[layer], load_sems.at[layer])
+        for layer in range(layers)
+    ]
+    for load in loads:
+        load.start()
+    row_peers, column_peers = around(down, along, n_down, n_along)
+    greet(row_peers + column_peers)
+    part = grad_probe.shape[0] // n_along
     piece = part // n_down
-    barrier = pltpu.get_barrier_semaphore()
-    row_peers = [(down, lax.rem(along + step, n_along)) for step in range(1, n_along)]
-    column_peers = [(lax.rem(down + step, n_down), along) for step in range(1, n_down)]
-    for peer in row_peers + column_peers:
-        pl.semaphore_signal(barrier, inc=1, device_id=peer, device_id_type=MESH)
-    pl.semaphore_wait(barrier, n_along + n_down - 2)
+    below, after = (lax.rem(down + 1, n_down), along), (down, lax.rem(along + 1, n_along))
+    not_top, not_bottom = down > 0, down < n_down - 1
+    not_first, not_last = along > 0, along < n_along - 1
 
     def exchange(index, source, target, peer):
-        copy = pltpu.make_async_remote_copy(
-            src_ref=source, dst_ref=target, send_sem=send_sems.at[index], recv_sem=recv_sems.at[index],
-            device_id=peer, device_id_type=MESH)
+        copy = remote(source, target, send_sems.at[index], recv_sems.at[index], peer)
         copy.start()
         return copy
 
-    def rows(start, size):
+    def aligned(start, size):
         return pl.ds(pl.multiple_of(start, 8), size)
 
-    copies = [
-        exchange(step, grad.at[rows(peer[1] * part, part)], from_row.at[step], peer)
-        for step, peer in enumerate(row_peers)
+    row_copies = [
+        exchange(step, grad_probe.at[aligned(peer[1] * part, part)], from_row.at[step], peer) for step, peer in enumerate(row_peers)
     ]
-    total = grad[rows(along * part, part)]
-    for step, copy in enumerate(copies):
+    base = 2 * (n_along + n_down - 2)
+    corners, sides, firsts, seconds, hops, forwards = [], [], [], [], [], []
+    half = n_down // 2
+    wraps, passes = down == half - 1, down == n_down - 1
+    over, down_three = (lax.rem(down + half, n_down), along), (lax.rem(down + n_down - 3, n_down), along)
+    for layer in range(layers):
+        at = base + 5 * layer
+        corners.append(remote(rights[layer].at[:, pl.ds(rows, points), :], corner_in.at[layer], send_sems.at[at], recv_sems.at[at], after))
+        sides.append(remote(rights[layer].at[:, pl.ds(0, rows), :], right_in.at[layer], send_sems.at[at + 1], recv_sems.at[at + 1], after))
+        rest = pl.ds(points, cols - points)
+        firsts.append(remote(lowers[layer].at[:, :, rest], lower_in.at[layer, :, :, rest], send_sems.at[at + 2], recv_sems.at[at + 2], below))
+        seconds.append(remote(held.at[layer], lower_in.at[layer, :, :, pl.ds(0, points)], send_sems.at[at + 3], recv_sems.at[at + 3], below))
+        hops.append(remote(lowers[layer].at[:, :, rest], relay.at[layer], send_sems.at[at + 4], recv_sems.at[at + 4], over))
+        forwards.append(remote(relay.at[layer], lower_in.at[layer, :, :, rest], send_sems.at[at + 2], recv_sems.at[at + 2], down_three))
+    for layer in range(layers):
+        when(not_bottom & not_last, corners[layer].start)
+
+    total = grad_probe[aligned(along * part, part)]
+    for step, copy in enumerate(row_copies):
         copy.wait()
         total = total + from_row[step]
     row_sum[...] = total
-    base = len(row_peers)
+    at = n_along - 1
     copies = [
-        exchange(base + step, row_sum.at[rows(peer[0] * piece, piece)], from_column.at[step], peer)
+        exchange(at + step, row_sum.at[aligned(peer[0] * piece, piece)], from_column.at[step], peer)
         for step, peer in enumerate(column_peers)
     ]
-    total = row_sum[rows(down * piece, piece)]
+    total = row_sum[aligned(down * piece, piece)]
     for step, copy in enumerate(copies):
         copy.wait()
         total = total + from_column[step]
-    mine = rows(along * part + down * piece, piece)
-    out[mine] = probe[mine] - total
-    base += len(column_peers)
-    copies = [exchange(base + step, out.at[mine], out.at[mine], peer) for step, peer in enumerate(column_peers)]
+    mine = aligned(along * part + down * piece, piece)
+    probe_out[mine] = probe[mine] - total
+    at += n_down - 1
+    copies = [exchange(at + step, probe_out.at[mine], probe_out.at[mine], peer) for step, peer in enumerate(column_peers)]
+    for layer in range(layers):
+        when(not_bottom & ~wraps, firsts[layer].start)
+        when(wraps, hops[layer].start)
     for copy in copies:
         copy.wait()
-    base += len(column_peers)
-    mine = rows(along * part, part)
-    copies = [exchange(base + step, out.at[mine], out.at[mine], peer) for step, peer in enumerate(row_peers)]
-    for copy in copies:
+    at += n_down - 1
+    mine = aligned(along * part, part)
+    row_copies = [exchange(at + step, probe_out.at[mine], probe_out.at[mine], peer) for step, peer in enumerate(row_peers)]
+
+    for layer in range(layers):
+        loads[layer].wait()
+        when(not_bottom & not_first, corners[layer].wait_recv)
+
+        @pl.when(not_bottom & not_first)
+        def _():
+            held[layer] += corner_in[layer]
+
+        when(not_bottom, seconds[layer].start)
+        when(not_last, sides[layer].start)
+    for layer in range(layers):
+        when(passes, hops[layer].wait_recv)
+        when(passes, forwards[layer].start)
+    for copy in row_copies:
         copy.wait()
-
-
-def update_probe(grad_probe, probe_wave, scale):
-    shape = probe_wave.shape
+    for layer in range(layers):
+        when(not_bottom & not_last, corners[layer].wait_send)
+        when(not_last, sides[layer].wait_send)
+        when(not_first, sides[layer].wait_recv)
+        when(not_bottom & ~wraps, firsts[layer].wait_send)
+        when(not_top, firsts[layer].wait_recv)
+        when(wraps, hops[layer].wait_send)
+        when(passes, forwards[layer].wait_send)
+        when(not_bottom, seconds[layer].wait_send)
+        when(not_top, seconds[layer].wait_recv)
+
+
+def send_back(rights, lowers, grad_probe, probe_wave, scale, rows):
     flat = (probe_wave.size // 128, 128)
     n_down, n_along = lax.axis_size("ty"), lax.axis_size("tx")
     part = flat[0] // n_along
     piece = part // n_down
-    copies = 2 * (n_along + n_down - 2)
+    layers = len(rights)
+    points = rights[0].shape[2]
+    cols = lowers[0].shape[2]
+    copies = 2 * (n_along + n_down - 2) + 5 * layers
     vmem = pl.BlockSpec(memory_space=pltpu.VMEM)
-    out = pl.pallas_call(
-        probe_kernel,
-        out_shape=jax.ShapeDtypeStruct(flat, jnp.float32),
-        in_specs=[vmem, vmem],
-        out_specs=vmem,
+    shape = lambda *dims: jax.ShapeDtypeStruct(dims, jnp.float32)
+    right_in, lower_in, probe = pl.pallas_call(
+        return_kernel,
+        out_shape=[shape(layers, 2, rows, points), shape(layers, 2, points, cols), shape(*flat)],
+        in_specs=[ANY] * (2 * layers) + [vmem, vmem],
+        out_specs=[ANY, ANY, vmem],
         scratch_shapes=[
+            pltpu.VMEM((layers, 2, points, points), jnp.float32),
+            pltpu.VMEM((layers, 2, points, points), jnp.float32),
+            pltpu.VMEM((layers, 2, points, cols - points), jnp.float32),
             pltpu.VMEM((n_along - 1, part, 128), jnp.float32),
             pltpu.VMEM((part, 128), jnp.float32),
             pltpu.VMEM((n_down - 1, piece, 128), jnp.float32),
+            pltpu.SemaphoreType.DMA((layers,)),
             pltpu.SemaphoreType.DMA((copies,)),
             pltpu.SemaphoreType.DMA((copies,)),
         ],
-        compiler_params=pltpu.CompilerParams(collective_id=1, has_side_effects=True),
-    )((grad_probe * scale).reshape(flat), probe_wave.reshape(flat))
-    return out.reshape(shape)
+        compiler_params=pltpu.CompilerParams(collective_id=1, has_side_effects=True, vmem_limit_bytes=VMEM_LIMIT),
+    )(*rights, *lowers, (grad_probe * scale).reshape(flat), probe_wave.reshape(flat))
+    return right_in, lower_in, probe.reshape(probe_wave.shape)
 
 
 def local(object_slab, probe_wave, frames, scan_tiles, scan_offsets):
@@ -401,28 +621,12 @@
     by_owner = scan_tiles.reshape(columns, owned)
 
     mine = lax.dynamic_index_in_dim(by_owner, col_index, 0, keepdims=False)
-    wanted = row_index * columns + jnp.arange(columns, dtype=jnp.int32)
+    other_row = lax.rem(row_index + lax.axis_size("ty") // 2, lax.axis_size("ty"))
+    places = jnp.arange(columns, dtype=jnp.int32)
+    wanted = jnp.concatenate([row_index * columns + places, other_row * columns + places])
     source = jnp.sum((mine[None, :] == wanted[:, None]).astype(jnp.int32) * jnp.arange(owned, dtype=jnp.int32)[None, :], axis=1)
 
-    def pick_kernel(source_ref, frames_ref, out_ref, sems):
-        copies = [
-            pltpu.make_async_copy(frames_ref.at[source_ref[place]], out_ref.at[place], sems.at[place])
-            for place in range(columns)
-        ]
-        for copy in copies:
-            copy.start()
-        for copy in copies:
-            copy.wait()
-
-    outgoing = pl.pallas_call(
-        pick_kernel,
-        out_shape=jax.ShapeDtypeStruct((columns, points, points), jnp.float32),
-        grid_spec=pltpu.PrefetchScalarGridSpec(
-            num_scalar_prefetch=1, grid=(1,), in_specs=[ANY], out_specs=ANY,
-            scratch_shapes=[pltpu.SemaphoreType.DMA((columns,))]),
-        cost_estimate=pl.CostEstimate(flops=0, bytes_accessed=8 * 1024 * 1024, transcendentals=0),
-    )(source, frames)
-    arrived = lax.all_to_all(outgoing, "tx", split_axis=0, concat_axis=0, tiled=True)
+    right, lower, corner, arrived = fetch(source, frames, object_slab, points)
 
     matches = by_owner == my_tile
     present = jnp.any(matches, axis=1)
@@ -435,13 +639,6 @@
     count = jnp.sum(present.astype(jnp.int32)).reshape(1)
     offsets = scan_offsets[chosen_ids].reshape(-1)
     scalars = (offsets, count, owners)
-
-    halos = []
-    for layer in range(layers):
-        right = passed_along(object_slab[layer, :, :, :points], "tx", -1)
-        lower = passed_along(object_slab[layer, :, :points, :], "ty", -1)
-        corner = passed_along(lower[:, :, :points], "tx", -1)
-        halos.append((right, lower, corner))
 
     spread_ahead, spread_back, fourier_ahead, fourier_back, shuffle = build_tables(points)
     slot_spec = pl.BlockSpec((1, 2, points, points), lambda slot, offsets, count, owners: (slot, 0, 0, 0))
@@ -457,28 +654,27 @@
     ]
 
     wave = call(
-        first_kernel, scalars, (object_slab, *halos[0], probe_wave, *spread_ahead),
+        first_kernel, scalars, (object_slab, right, lower, corner, probe_wave, *spread_ahead),
         [ANY] * 4 + [whole(probe_wave)] + [whole(t) for t in spread_ahead],
         waves, slot_spec, [canvas, sems], flops)
     grad_wave, *grad_one = call(
-        second_kernel, scalars, (object_slab, *halos[1], wave, arrived, *fourier_ahead, *fourier_back, shuffle),
+        second_kernel, scalars, (object_slab, right, lower, corner, wave, arrived, *fourier_ahead, *fourier_back, shuffle),
         [ANY] * 4 + [slot_spec, frame_spec] + [whole(t) for t in (*fourier_ahead, *fourier_back, shuffle)],
         [waves] + grads, [slot_spec] + [ANY] * 3, [canvas, canvas, sems, pltpu.VMEM((points // 128, points, 128), jnp.float32)], 2 * flops)
     grad_probe, *grad_zero = call(
-        third_kernel, scalars, (object_slab, *halos[0], probe_wave, grad_wave, *spread_back),
+        third_kernel, scalars, (object_slab, right, lower, corner, probe_wave, grad_wave, *spread_back),
         [ANY] * 4 + [whole(probe_wave), slot_spec] + [whole(t) for t in spread_back],
         [jax.ShapeDtypeStruct(probe_wave.shape, jnp.float32)] + grads,
         [whole(probe_wave)] + [ANY] * 3, [canvas, canvas, sems], flops)
 
-    totals = []
-    for tile, right, lower in (grad_zero, grad_one):
-        right_back = passed_along(right, "tx", 1)
-        lower = lower.at[:, :, :points].add(right_back[:, tile_rows:])
-        lower_back = passed_along(lower, "ty", 1)
-        tile = tile.at[:, :, :points].add(right_back[:, :tile_rows])
-        totals.append(tile.at[:, :points, :].add(lower_back))
-    new_probe = update_probe(grad_probe, probe_wave, PROBE_RATE / total_frames)
-    return (object_slab - OBJECT_RATE * jnp.stack(totals), new_probe)
+    right_back, lower_back, new_probe = send_back(
+        [grad_zero[1], grad_one[1]], [grad_zero[2], grad_one[2]], grad_probe, probe_wave, PROBE_RATE / total_frames, tile_rows)
+    right_back = jnp.where(col_index > 0, right_back, 0.0)
+    lower_back = jnp.where(row_index > 0, lower_back, 0.0)
+    total = jnp.stack([grad_zero[0], grad_one[0]])
+    total = total + jnp.pad(right_back, ((0, 0), (0, 0), (0, 0), (0, tile_cols - points)))
+    total = total + jnp.pad(lower_back, ((0, 0), (0, 0), (0, tile_rows - points), (0, 0)))
+    return (object_slab - OBJECT_RATE * total, new_probe)
 
 
 def solution(mesh):

time: 417 us -> 266 us (0.64); the launches traced: 412 us -> 266 us
  waiting for transfers between devices: 88.7 us -> 0 us
  starting transfers between devices: 40.7 us -> 0 us
  local copies, waits for them, and re-layouts: 16.2 us -> 5.64 us
    ppermute x10 -> x0, waiting for transfers between devices: 88.7 us -> none  [passed_along(): lax.ppermute(value, axis, [(source, source + steps) for source in range(l...]
    ppermute x10 -> x0, starting transfers between devices: 34.9 us -> none  [passed_along(): lax.ppermute(value, axis, [(source, source + steps) for source in range(l...]
    pallas_call x3, Pallas kernels: 65.5 us -> 50.8 us  [call(): pl.pallas_call(kernel, out_shape=out_shapes, grid_spec=pltpu.PrefetchScal...]
    pallas_call x2, Pallas kernels: 183 us -> 195 us  [the longest x1 109 us: send_back(): pl.pallas_call(return_kernel, out_shape=[shape(layers, 2, rows, points),...]
    scatter-add x6 -> x0, other arithmetic: 9.18 us -> none  [the longest x2 4.39 us: local(): lower = lower.at[:, :, :points].add(right_back[:, tile_rows:])]
    all_to_all x1 -> x0, starting transfers between devices: 5.85 us -> none  [local(): lax.all_to_all(outgoing, 'tx', split_axis=0, concat_axis=0, tiled=True)]
    squeeze x2 -> x0, local copies, waits for them, and re-layouts: 4.55 us -> none  [the longest x1 2.91 us: local(): lower = passed_along(object_slab[layer, :, :points, :], 'ty', -1)]
  transfers between devices with their start and end apart: 11 -> 0, of which waited for: 4 -> 0; matrix products, arithmetic and copies ran while one was open for 6% -> 0% of each run, Pallas kernels for 17% -> 0%
where the time goes in v2:
time: 266 us
  Pallas kernels  246 us (92%)
  other arithmetic  13.3 us (5%)
  local copies, waits for them, and re-layouts  5.64 us (2%)
    pallas_call x1, Pallas kernels, send_back(): pl.pallas_call(return_kernel, out_shape=[shape(layers, 2, rows, points),...  109 us
    pallas_call x1, Pallas kernels, fetch(): pl.pallas_call(fetch_kernel, out_shape=[shape(layers, 2, rows, points), s...  86.1 us
    pallas_call x3, Pallas kernels, call(): pl.pallas_call(kernel, out_shape=out_shapes, grid_spec=pltpu.PrefetchScal...  50.8 us
    sub x1, other arithmetic, local(): return (object_slab - OBJECT_RATE * total, new_probe)  5.75 us

profile of v2, /device:TPU:104, one launch (start us, length us, event | category | flops | bytes accessed | tf_op | source)
XLA Modules:
  0.0 265.9 jit_solution(2175209965424836351)
XLA Ops:
  0.6 0.1 pad_add_fusion
  0.7 0.8 reshape.76
  1.5 0.7 select_reduce_fusion.source
  2.2 0.0 copy-start.3
  2.2 86.1 %shard_map.221 = (f32[2,2,512,256]{3,2,1,0:T(8,128)}, f32[2,2,256,512]{3,2,1,0:T(8,128)}, f32[2,2,256,256]{3,2,1,0:T(8,128)}, f32[16,256,256]{2,1,0:T(8,128)}) custom-call(s32[32]{0:T(128)} %select_reduce_fusion.source, f32[48,256,256]{2,1,0:T(8,128)} %frames.1, f32[2,2,512,512]{3,2,1,0:T(8,128)} %tile.5), custom_call_target="tpu_custom_call" | custom-call | tf_op jit(solution)/shard_map/pallas_call | solution.py:458
  88.3 0.1 select_reduce_fusion.1
  88.4 0.1 reduce_or.9
  88.6 0.1 copy.28
  88.7 0.1 add_reduce_fusion
  88.8 0.7 select_reduce_fusion.2
  89.5 0.0 copy-done.3
  89.5 0.2 copy.29
  89.7 0.6 gather_fusion
  90.3 0.6 reshape.77.offsets
  90.9 0.7 convert_reduce_fusion
  91.6 12.3 %shard_map.222.wave = f32[8,2,256,256]{3,2,1,0:T(8,128)} custom-call(s32[16]{0:T(128)} %reshape.77.offsets, s32[1]{0:T(128)} %bitcast.3.count, s32[8]{0:T(128)} %get-tuple-element.32.owners, f32[2,2,512,512]{3,2,1,0:T(8,128)} %tile.5, f32[2,2,512,256]{3,2,1,0:T(8,128)} %get-tuple-element.17.right, f32[2,2,256,512]{3,2,1,0:T(8,128)} %get-tuple-element.18.lower, ...), custom_call_target="tpu_custom_call" | custom-call | flops 3221225472 | bytes 16777216 | tf_op jit(solution)/shard_map/pallas_call | solution.py:305
  103.9 22.8 %shard_map.223 = (f32[8,2,256,256]{3,2,1,0:T(8,128)}, f32[2,512,512]{2,1,0:T(8,128)}, f32[2,768,256]{2,1,0:T(8,128)}, f32[2,256,512]{2,1,0:T(8,128)}) custom-call(s32[16]{0:T(128)} %reshape.77.offsets, s32[1]{0:T(128)} %bitcast.3.count, s32[8]{0:T(128)} %get-tuple-element.32.owners, f32[2,2,512,512]{3,2,1,0:T(8,128)} %tile.5, ...), custom_call_target="tpu_custom_call" | custom-call | flops 6442450944 | bytes 16777216 | tf_op jit(solution)/shard_map/pallas_call | solution.py:305
  126.7 15.8 %shard_map.224 = (f32[2,256,256]{2,1,0:T(8,128)}, f32[2,512,512]{2,1,0:T(8,128)}, f32[2,768,256]{2,1,0:T(8,128)}, f32[2,256,512]{2,1,0:T(8,128)}) custom-call(s32[16]{0:T(128)} %reshape.77.offsets, s32[1]{0:T(128)} %bitcast.3.count, s32[8]{0:T(128)} %get-tuple-element.32.owners, f32[2,2,512,512]{3,2,1,0:T(8,128)} %tile.5, ...), custom_call_target="tpu_custom_call" | custom-call | flops 3221225472 | bytes 16777216 | tf_op jit(solution)/shard_map/pallas_call | solution.py:305
  142.5 0.0 copy-start.1
  142.5 1.1 broadcast_multiply_fusion
  143.6 0.8 reshape.79.grad_probe
  144.4 0.0 copy-done.1
  144.5 0.8 reshape.80.probe
  145.3 109.3 %shard_map.225 = (f32[2,2,512,256]{3,2,1,0:T(8,128)}, f32[2,2,256,512]{3,2,1,0:T(8,128)}, f32[1024,128]{1,0:T(8,128)}) custom-call(f32[2,768,256]{2,1,0:T(8,128)} %get-tuple-element.24.right_0, f32[2,768,256]{2,1,0:T(8,128)} %get-tuple-element.25.right_1, f32[2,256,512]{2,1,0:T(8,128)} %get-tuple-element.26.lower_0, ...), custom_call_target="tpu_custom_call" | custom-call | tf_op jit(solution)/shard_map/pallas_call | solution.py:591
  254.6 1.8 broadcast_select_fusion.1
  256.4 0.0 copy-start
  256.4 2.0 broadcast_select_fusion
  258.4 0.8 copy-done
  259.2 0.0 copy-start.2
  259.2 5.7 %fusion.2 = f32[2,2,512,512]{3,2,1,0:T(8,128)} fusion(f32[2,2,512,512]{3,2,1,0:T(8,128)S(1)} %copy-done, f32[1,2,512,512]{3,2,1,0:T(8,128)} %bitcast.11, f32[1,2,512,512]{3,2,1,0:T(8,128)} %bitcast.12, f32[2,2,256,512]{3,2,1,0:T(8,128)S(1)} %broadcast_select_fusion, f32[2,2,512,256]{3,2,1,0:T(8,128)S(1)} %broadcast_select_fusion.1), kind=kLoop, calls=%fused_computation.4 | loop fusion | flops 5242880 | bytes 16777216 | tf_op jit(solution)/shard_map/sub | solution.py:677
  265.0 0.0 copy-done.2
  265.0 0.9 reshape.81
  (7 shorter events, 0.1 us)
Async XLA Ops:
  2.2 87.3 %copy-start.3 = (s32[768,2]{0,1:T(2,128)S(1)}, s32[768,2]{0,1:T(2,128)}, u32[]{:S(2)}) copy-start(s32[768,2]{0,1:T(2,128)} %param.26) | copy-start | bytes 18436
  142.5 2.0 copy-start.1
  256.4 2.8 %copy-start = (f32[2,2,512,512]{3,2,1,0:T(8,128)S(1)}, f32[2,2,512,512]{3,2,1,0:T(8,128)}, u32[]{:S(2)}) copy-start(f32[2,2,512,512]{3,2,1,0:T(8,128)} %tile.5) | copy-start | bytes 12582916
  259.2 5.8 %copy-start.2 = (f32[1024,128]{1,0:T(8,128)S(1)}, f32[1024,128]{1,0:T(8,128)}, u32[]{:S(2)}) copy-start(f32[1024,128]{1,0:T(8,128)} %get-tuple-element.31) | copy-start | bytes 1572868

commit v3 on v2

v3 whole, which is shorter than its diff:
```python
import functools
import math

import jax
import jax.numpy as jnp
import ml_dtypes
import numpy as np
from jax import lax
from jax.experimental import pallas as pl
from jax.experimental.pallas import tpu as pltpu
from jax.sharding import PartitionSpec as P

MESH = pl.DeviceIdType.MESH
TILE_CAP = 8
HOPS = 4
BACKGROUND = 0.5
FRESNEL = 0.25
OBJECT_RATE = 0.25
PROBE_RATE = 4.0
VMEM_LIMIT = 56 * 1024 * 1024


FRAME_STEPS = ((1, 0, 0), (3, 0, 0), (0, 1, 1), (2, 0, 0), (1, 1, 1), (3, 1, 1), (0, 1, 0), (2, 1, 1), (1, 0, 1), (3, 0, 1), (2, 0, 1),
               (1, 1, 0), (3, 1, 0), (2, 1, 0), (0, 0, 1))


def real_form(matrix):
    return np.block([[matrix.real, -matrix.imag], [matrix.imag, matrix.real]])


def split_table(table):
    high = table.astype(ml_dtypes.bfloat16)
    low = (table - high.astype(np.float64)).astype(ml_dtypes.bfloat16)
    return high, low


def left_table(table):
    return np.concatenate(split_table(table), axis=1)


def right_table(table):
    return np.concatenate(split_table(table), axis=0)


def half_transforms(points):
    half = points // 2
    places = np.arange(half)
    even = np.exp(-2j * np.pi * ((2 * places[:, None]) * places[None, :] % points) / points)
    odd = np.exp(-2j * np.pi * ((2 * places[:, None] + 1) * places[None, :] % points) / points)
    return even / math.sqrt(points), odd / math.sqrt(points)


def build_tables(points):
    even, odd = half_transforms(points)
    places = np.arange(points)
    frequency = (places + points // 2) % points - points // 2
    phase = np.exp(-1j * np.pi * FRESNEL / points * frequency.astype(np.float64) ** 2)
    spread_even = even.conj().T @ (phase[0::2, None] * even)
    spread_odd = odd.conj().T @ (phase[1::2, None] * odd)
    spread = [real_form(spread_even), real_form(spread_odd)]
    fourier = [real_form(even), real_form(odd)]
    order = np.concatenate([places[0::2], places[1::2]])
    shuffle = (places[:, None] == order[None, :]).astype(ml_dtypes.bfloat16)

    groups = [spread, [table.T for table in spread], fourier, [table.T for table in fourier]]
    left = np.stack([left_table(table) for group in groups for table in group])
    right = np.stack([right_table(table.T) for group in groups for table in group])
    return left, right, shuffle


def split(value):
    high = value.astype(jnp.bfloat16)
    low = (value - high.astype(jnp.float32)).astype(jnp.bfloat16)
    return high, low


def left_product(table, value):
    high, low = split(value)
    size = value.shape[0]
    table = jnp.concatenate([table[...], table[:, :size]], axis=1)
    return jnp.dot(table, jnp.concatenate([high, high, low], axis=0), preferred_element_type=jnp.float32)


def right_product(value, table):
    high, low = split(value)
    size = value.shape[1]
    table = jnp.concatenate([table[...], table[:size, :]], axis=0)
    return jnp.dot(jnp.concatenate([high, high, low], axis=1), table, preferred_element_type=jnp.float32)


def halves(value, axis):
    half = value.shape[axis] // 2
    first = lax.slice_in_dim(value, 0, half, axis=axis)
    second = lax.slice_in_dim(value, half, 2 * half, axis=axis)
    return first, second


def apart(real, imag, axis):
    real_a, real_b = halves(real, axis)
    imag_a, imag_b = halves(imag, axis)
    plus = jnp.concatenate([real_a + real_b, imag_a + imag_b], axis=axis)
    minus = jnp.concatenate([real_a - real_b, imag_a - imag_b], axis=axis)
    return plus, minus


def together(plus, minus, axis):
    plus_re, plus_im = halves(plus, axis)
    minus_re, minus_im = halves(minus, axis)
    real = jnp.concatenate([plus_re + minus_re, plus_re - minus_re], axis=axis)
    imag = jnp.concatenate([plus_im + minus_im, plus_im - minus_im], axis=axis)
    return real, imag


def regroup(even, odd, axis):
    even_re, even_im = halves(even, axis)
    odd_re, odd_im = halves(odd, axis)
    return jnp.concatenate([even_re, odd_re], axis=axis), jnp.concatenate([even_im, odd_im], axis=axis)


def spread(real, imag, tables):
    left_even, left_odd, right_even, right_odd = tables
    plus, minus = apart(real, imag, 0)
    real, imag = together(left_product(left_even, plus), left_product(left_odd, minus), 0)
    plus, minus = apart(real, imag, 1)
    return together(right_product(plus, right_even), right_product(minus, right_odd), 1)


def to_frequencies(real, imag, tables):
    left_even, left_odd, right_even, right_odd = tables
    plus, minus = apart(real, imag, 0)
    real, imag = regroup(left_product(left_even, plus), left_product(left_odd, minus), 0)
    plus, minus = apart(real, imag, 1)
    return regroup(right_product(plus, right_even), right_product(minus, right_odd), 1)


def from_frequencies(real, imag, tables):
    left_even, left_odd, right_even, right_odd = tables
    even, odd = regroup(real, imag, 0)
    real, imag = together(left_product(left_even, even), left_product(left_odd, odd), 0)
    even, odd = regroup(real, imag, 1)
    return together(right_product(even, right_even), right_product(odd, right_odd), 1)


def place_of(row, column, points):
    return pl.ds(row, points), column // 128, lax.rem(column, 128)


def window_of(canvas, layer, place, points):
    rows, first, along = place
    before = lax.broadcasted_iota(jnp.int32, (points, 128), 1) < 128 - along
    parts = []
    for part in range(2):
        turned = [
            pltpu.roll(canvas[layer, part, first + step, rows, :], lax.rem(128 - along, 128), 1)
            for step in range(points // 128 + 1)
        ]
        parts.append(jnp.concatenate([jnp.where(before, one, other) for one, other in zip(turned, turned[1:])], axis=1))
    return parts


def add_window(canvas, layer, place, points, parts):
    rows, first, along = place
    inside = lax.broadcasted_iota(jnp.int32, (points, 128), 1) >= along
    for part in range(2):
        turned = [pltpu.roll(parts[part][:, at:at + 128], along, 1) for at in range(0, points, 128)]
        none = jnp.zeros((points, 128), jnp.float32)
        for step, (one, other) in enumerate(zip(turned + [none], [none] + turned)):
            canvas[layer, part, first + step, rows, :] += jnp.where(inside, one, other)


def times(a, b):
    return a[0] * b[0] - a[1] * b[1], a[0] * b[1] + a[1] * b[0]


def times_conjugate(a, b):
    return a[0] * b[0] + a[1] * b[1], a[0] * b[1] - a[1] * b[0]


def gradient_kernel(offsets, count, owners, slab, right, lower, corner, arrived, probe, left_all, right_all, shuffle_all, moved,
                    grad_right, grad_lower, grad_probe, canvas, grad, frame, columns, left_held, right_held, shuffle, load_sems,
                    table_sems, frame_sems, out_sems):
    table_loads = [
        pltpu.make_async_copy(source, target, table_sems.at[at])
        for at, (source, target) in enumerate(((left_all, left_held), (right_all, right_held), (shuffle_all, shuffle)))
    ]
    spread_ahead, spread_back, fourier_ahead, fourier_back = (
        [left_held.at[at], left_held.at[at + 1], right_held.at[at], right_held.at[at + 1]] for at in range(0, 8, 2))
    layers, rows, cols = slab.shape[0], slab.shape[2], slab.shape[3]
    points = probe.shape[1]
    half = points // 2
    own_lanes, more_lanes = cols // 128, points // 128
    own, beside = pl.ds(0, rows), pl.ds(rows, points)

    def lanes(number):
        return pl.ds(128 * number, 128)

    def frame_copy(slot):
        return pltpu.make_async_copy(arrived.at[owners[slot]], frame.at[lax.rem(slot, 2)], frame_sems.at[lax.rem(slot, 2)])

    pairs = []
    for layer in range(layers):
        for number in range(own_lanes):
            pairs.append((slab.at[layer, :, :, lanes(number)], canvas.at[layer, :, number, own, :]))
            pairs.append((lower.at[layer, :, :, lanes(number)], canvas.at[layer, :, number, beside, :]))
        for number in range(more_lanes):
            pairs.append((right.at[layer, :, :, lanes(number)], canvas.at[layer, :, own_lanes + number, own, :]))
            pairs.append((corner.at[layer, :, :, lanes(number)], canvas.at[layer, :, own_lanes + number, beside, :]))
    loads = [pltpu.make_async_copy(source, target, load_sems.at[at]) for at, (source, target) in enumerate(pairs)]
    for load in loads + table_loads:
        load.start()

    @pl.when(count[0] > 0)
    def _():
        frame_copy(0).start()

    grad[...] = jnp.zeros_like(grad)
    grad_probe[...] = jnp.zeros_like(grad_probe)
    for load in loads + table_loads:
        load.wait()

    @pl.when(lax.axis_index("ty") == lax.axis_size("ty") - 1)
    def _():
        canvas[:, :, :, beside, :] = jnp.zeros((layers, 2, own_lanes + more_lanes, points, 128), jnp.float32)

    @pl.when(lax.axis_index("tx") == lax.axis_size("tx") - 1)
    def _():
        canvas[:, :, pl.ds(own_lanes, more_lanes)] = jnp.zeros((layers, 2, more_lanes, rows + points, 128), jnp.float32)

    def visit(slot, carry):
        place = place_of(offsets[2 * slot], offsets[2 * slot + 1], points)
        frame_copy(slot).wait()

        @pl.when(slot + 1 < count[0])
        def _():
            frame_copy(slot + 1).start()

        probe_wave = (probe[0], probe[1])
        windows = [window_of(canvas, layer, place, points) for layer in range(layers)]
        wave = spread(*times(probe_wave, windows[0]), spread_ahead)
        real, imag = to_frequencies(*times(wave, windows[1]), fourier_ahead)
        pieces = []
        for side in range(points // 128):
            columns[side] = jnp.sqrt(frame[lax.rem(slot, 2), :, pl.ds(side * 128, 128)] + BACKGROUND)
            pieces.append(jnp.concatenate([columns[side, pl.ds(start, half, stride=2), :] for start in range(2)], axis=0))
        target = jnp.concatenate(pieces, axis=1)
        high = target.astype(jnp.bfloat16)
        rest = target - high.astype(jnp.float32)
        middle = rest.astype(jnp.bfloat16)
        low = (rest - middle.astype(jnp.float32)).astype(jnp.bfloat16)
        target = jnp.dot(
            jnp.concatenate([high, middle, low], axis=1), jnp.concatenate([shuffle[...]] * 3, axis=0),
            preferred_element_type=jnp.float32)
        pull = 2.0 - 2.0 * target * lax.rsqrt(real * real + imag * imag + BACKGROUND)
        back = from_frequencies(pull * real, pull * imag, fourier_back)
        add_window(grad, 1, place, points, times_conjugate(wave, back))
        back = times_conjugate(windows[1], back)
        back = spread(*back, spread_back)
        add_window(grad, 0, place, points, times_conjugate(probe_wave, back))
        more = times_conjugate(windows[0], back)
        grad_probe[0] += more[0]
        grad_probe[1] += more[1]
        return carry

    lax.fori_loop(0, count[0], visit, 0)
    writes = [
        pltpu.make_async_copy(grad.at[:, :, own_lanes + number], grad_right.at[:, :, :, lanes(number)], out_sems.at[number])
        for number in range(more_lanes)
    ]
    writes += [
        pltpu.make_async_copy(grad.at[:, :, number, beside, :], grad_lower.at[:, :, :, lanes(number)], out_sems.at[more_lanes + number])
        for number in range(own_lanes)
    ]
    for write in writes:
        write.start()
    for number in range(own_lanes):
        canvas[:, :, number, :rows, :] -= OBJECT_RATE * grad[:, :, number, :rows, :]
        writes.append(pltpu.make_async_copy(
            canvas.at[:, :, number, own, :], moved.at[:, :, :, lanes(number)], out_sems.at[more_lanes + own_lanes + number]))
        writes[-1].start()
    for write in writes:
        write.wait()


ANY = pl.BlockSpec(memory_space=pl.ANY)
WHOLE = pl.BlockSpec(memory_space=pltpu.VMEM)


def gradients(scalars, object_slab, right, lower, corner, arrived, probe_wave):
    layers, _, rows, cols = object_slab.shape
    points = probe_wave.shape[-1]
    tables = build_tables(points)
    shape = lambda *dims: jax.ShapeDtypeStruct(dims, jnp.float32)
    canvas = pltpu.VMEM((layers, 2, (cols + points) // 128, rows + points, 128), jnp.float32)
    lanes = (cols + points) // 128
    return pl.pallas_call(
        gradient_kernel,
        out_shape=[shape(*object_slab.shape), shape(layers, 2, rows + points, points), shape(layers, 2, points, cols),
                   shape(*probe_wave.shape)],
        grid_spec=pltpu.PrefetchScalarGridSpec(
            num_scalar_prefetch=len(scalars),
            grid=(1,),
            in_specs=[ANY] * 5 + [WHOLE] + [ANY] * len(tables),
            out_specs=[ANY] * 3 + [WHOLE],
            scratch_shapes=[
                canvas, canvas,
                pltpu.VMEM((2, points, points), jnp.float32),
                pltpu.VMEM((points // 128, points, 128), jnp.float32),
                *[pltpu.VMEM(table.shape, jnp.bfloat16) for table in tables],
                pltpu.SemaphoreType.DMA((2 * layers * lanes,)),
                pltpu.SemaphoreType.DMA((len(tables),)),
                pltpu.SemaphoreType.DMA((2,)),
                pltpu.SemaphoreType.DMA((lanes + cols // 128,)),
            ]),
        compiler_params=pltpu.CompilerParams(vmem_limit_bytes=VMEM_LIMIT),
        cost_estimate=pl.CostEstimate(flops=TILE_CAP * 96 * points**3, bytes_accessed=32 * 1024 * 1024, transcendentals=0),
    )(*scalars, object_slab, right, lower, corner, arrived, probe_wave, *tables)


def finish_kernel(moved, right, lower, out):
    points = right.shape[3]
    out[...] = moved[...]

    @pl.when(lax.axis_index("tx") > 0)
    def _():
        out[0, 0, :, :points] -= OBJECT_RATE * right[0, 0]

    @pl.when(lax.axis_index("ty") > 0)
    def _():
        out[0, 0, :points, :] -= OBJECT_RATE * lower[0, 0]


def finish(moved, right, lower):
    plane = lambda array: pl.BlockSpec((1, 1) + array.shape[2:], lambda layer, part: (layer, part, 0, 0))
    return pl.pallas_call(
        finish_kernel,
        out_shape=jax.ShapeDtypeStruct(moved.shape, moved.dtype),
        grid=moved.shape[:2],
        in_specs=[plane(moved), plane(right), plane(lower)],
        out_specs=plane(moved),
        compiler_params=pltpu.CompilerParams(vmem_limit_bytes=VMEM_LIMIT),
        cost_estimate=pl.CostEstimate(flops=3 * moved.size, bytes_accessed=12 * moved.size, transcendentals=0),
    )(moved, right, lower)


def remote(source, target, send_sem, recv_sem, peer):
    return pltpu.make_async_remote_copy(
        src_ref=source, dst_ref=target, send_sem=send_sem, recv_sem=recv_sem, device_id=peer, device_id_type=MESH)


def when(condition, action):
    pl.when(condition)(lambda: action())


def greet(peers):
    barrier = pltpu.get_barrier_semaphore()
    for peer in peers:
        pl.semaphore_signal(barrier, inc=1, device_id=peer, device_id_type=MESH)
    pl.semaphore_wait(barrier, len(peers))


def around(down, along, n_down, n_along):
    row = [(down, lax.rem(along + step, n_along)) for step in range(1, n_along)]
    column = [(lax.rem(down + step, n_down), along) for step in range(1, n_down)]
    return row, column


def frame_peer(down, along, n_down, n_along, step, ahead):
    step_y, step_z, step_core = step
    if not ahead:
        step_y = -step_y % (n_along // 4)
    place_y, place_z, core = along // 4, lax.rem(along // 2, 2), lax.rem(along, 2)
    other = step_z * jnp.maximum(step_core, core)
    place_y = lax.rem(place_y + step_y, n_along // 4)
    place_z = lax.rem(place_z + step_z, 2)
    core = lax.rem(core + step_core, 2)
    return (lax.rem(down + other * (n_down // 2), n_down), place_y * 4 + place_z * 2 + core), other


def fetch_kernel(source, frames, slab, right, lower, corner, arrived, held, picked, lower_relay, right_relay, held_sem, own_sem,
                 send_sems, recv_sems):
    down, along = lax.axis_index("ty"), lax.axis_index("tx")
    n_down, n_along = lax.axis_size("ty"), lax.axis_size("tx")
    layers, points, rows, cols = right.shape[0], right.shape[3], right.shape[2], lower.shape[3]
    half = n_down // 2
    load = pltpu.make_async_copy(frames, held, held_sem)
    load.start()
    ring = lambda by_down, by_along: (lax.rem(down + by_down + n_down, n_down), lax.rem(along + by_along + n_along, n_along))
    greet([frame_peer(down, along, n_down, n_along, step, False)[0] for step in FRAME_STEPS]
          + [ring(by, 0) for by in (1, -1, half, 3, -3)] + [ring(0, by) for by in (1, -1, 3, -3, 4, -4)])
    above, left = ring(-1, 0), ring(0, -1)
    not_top, not_bottom = down > 0, down < n_down - 1
    not_first, not_last = along > 0, along < n_along - 1
    wraps, passes = down == half, down == 0
    crosses, carries = lax.rem(along, 4) == 0, lax.rem(along, 4) == 3
    crossed = carries & not_last
    across = crosses & not_first
    base = n_along - 1
    index = iter(range(base, base + 64))

    def copy(source_ref, target, peer, at=None):
        at = next(index) if at is None else at
        return remote(source_ref, target, send_sems.at[at], recv_sems.at[at], peer)

    first, last = 0, layers - 1
    side = [slab.at[layer, :, :, pl.ds(0, points)] for layer in range(layers)]
    edge = [lower.at[layer, :, :, pl.ds(0, points)] for layer in range(layers)]
    rest, start = pl.ds(points, cols - points), pl.ds(0, points)
    lowers, others, hops, forwards, rights, corners = [], [], [], [], [], []
    for layer in range(layers):
        lowers.append(copy(slab.at[layer, :, pl.ds(0, points), start], lower.at[layer, :, :, start], above))
        at = next(index)
        others.append(copy(slab.at[layer, :, pl.ds(0, points), rest], lower.at[layer, :, :, rest], above, at))
        chunk = points // HOPS
        for number in range(HOPS):
            here = pl.ds(number * chunk, chunk)
            hop_at = next(index)
            hops.append(copy(slab.at[layer, :, here, rest], lower_relay.at[layer, :, here, :], ring(half, 0), hop_at))
            forwards.append(remote(
                lower_relay.at[layer, :, here, :], lower.at[layer, :, here, rest], send_sems.at[hop_at], recv_sems.at[at], ring(3, 0)))
        rights.append(copy(side[layer], right.at[layer], left))
        corners.append(copy(edge[layer], corner.at[layer], left))
    per_layer = 4 + HOPS
    at_right, at_corner = base + per_layer * layers - 2, base + per_layer * layers - 1
    right_hop = copy(side[last], right_relay.at[:, pl.ds(0, rows), :], ring(0, 3))
    right_forward = copy(right_relay.at[:, pl.ds(0, rows), :], right.at[last], ring(0, -4), at_right)
    corner_hop = copy(edge[last], right_relay.at[:, pl.ds(rows, points), :], ring(0, 3))
    corner_forward = copy(right_relay.at[:, pl.ds(rows, points), :], corner.at[last], ring(0, -4), at_corner)

    for layer in range(layers):
        when(not_top, lowers[layer].start)
        when(not_top & ~wraps, others[layer].start)
    when(across, right_hop.start)
    when(not_first & ~crosses, rights[last].start)
    when(not_first, rights[first].start)
    load.wait()
    sends = []
    for step, offset in enumerate(FRAME_STEPS):
        peer, other = frame_peer(down, along, n_down, n_along, offset, True)
        picked[step] = held[source[other * n_along + peer[1]]]
        send = remote(picked.at[step], arrived.at[along], send_sems.at[step], recv_sems.at[step], peer)
        send.start()
        sends.append(send)
    for hop in hops:
        when(wraps, hop.start)
    picked[n_along - 1] = held[source[along]]
    own = pltpu.make_async_copy(picked.at[n_along - 1], arrived.at[along], own_sem)
    own.start()
    relays = along >= 4
    for hop, forward in zip(hops, forwards):
        when(passes, hop.wait_recv)
        when(passes, forward.start)
    when(carries & relays, right_hop.wait_recv)
    when(carries & relays, right_forward.start)
    for layer in range(layers):
        when(not_bottom, lowers[layer].wait_recv)
        if layer == last:
            when(not_bottom & across, corner_hop.start)
            when(not_bottom & not_first & ~crosses, corners[layer].start)
            when(not_bottom & carries & relays, corner_hop.wait_recv)
            when(not_bottom & carries & relays, corner_forward.start)
        else:
            when(not_bottom & not_first, corners[layer].start)
    for layer in range(layers):
        when(not_bottom, others[layer].wait_recv)
        when(not_last, rights[layer].wait_recv)
        when(not_bottom & not_last, corners[layer].wait_recv)
        when(not_top, lowers[layer].wait_send)
        when(not_top & ~wraps, others[layer].wait_send)
        if layer == last:
            when(across, right_hop.wait_send)
            when(not_first & ~crosses, rights[layer].wait_send)
            when(carries & relays, right_forward.wait_send)
            when(not_bottom & across, corner_hop.wait_send)
            when(not_bottom & not_first & ~crosses, corners[layer].wait_send)
            when(not_bottom & carries & relays, corner_forward.wait_send)
        else:
            when(not_first, rights[layer].wait_send)
            when(not_bottom & not_first, corners[layer].wait_send)
    for hop, forward in zip(hops, forwards):
        when(wraps, hop.wait_send)
        when(passes, forward.wait_send)
    for send in sends:
        send.wait()
    own.wait()


def fetch(source, frames, object_slab, points):
    layers, _, rows, cols = object_slab.shape
    n_along = lax.axis_size("tx")
    copies = n_along - 1 + (4 + HOPS) * layers + 2
    shape = lambda *dims: jax.ShapeDtypeStruct(dims, jnp.float32)
    return pl.pallas_call(
        fetch_kernel,
        out_shape=[shape(layers, 2, rows, points), shape(layers, 2, points, cols), shape(layers, 2, points, points),
                   shape(n_along, points, points)],
        in_specs=[pl.BlockSpec(memory_space=pltpu.SMEM), ANY, ANY],
        out_specs=[ANY] * 4,
        scratch_shapes=[
            pltpu.VMEM(frames.shape, jnp.float32),
            pltpu.VMEM((n_along, points, points), jnp.float32),
            pltpu.VMEM((layers, 2, points, cols - points), jnp.float32),
            pltpu.VMEM((2, rows + points, points), jnp.float32),
            pltpu.SemaphoreType.DMA,
            pltpu.SemaphoreType.DMA,
            pltpu.SemaphoreType.DMA((copies,)),
            pltpu.SemaphoreType.DMA((copies,)),
        ],
        compiler_params=pltpu.CompilerParams(collective_id=0, has_side_effects=True, vmem_limit_bytes=VMEM_LIMIT),
    )(source, frames, object_slab)


def return_kernel(scale, all_right, all_lower, grad_probe, probe, right_in, lower_in, probe_out,
                  corner_in, held, relay, from_row, row_sum, from_column, load_sems, send_sems, recv_sems):
    down, along = lax.axis_index("ty"), lax.axis_index("tx")
    n_down, n_along = lax.axis_size("ty"), lax.axis_size("tx")
    rights, lowers = ([ref.at[layer] for layer in range(ref.shape[0])] for ref in (all_right, all_lower))
    layers, points, rows, cols = len(rights), right_in.shape[3], right_in.shape[2], lower_in.shape[3]
    loads = [
        pltpu.make_async_copy(lowers[layer].at[:, :, pl.ds(0, points)], held.at[layer], load_sems.at[layer])
        for layer in range(layers)
    ]
    for load in loads:
        load.start()
    row_peers, column_peers = around(down, along, n_down, n_along)
    greet(row_peers + column_peers)
    part = grad_probe.shape[0] // n_along

    def piece_of(number, start):
        return pl.ds(pl.multiple_of(start + number // 2 * 8, 8), 8), pl.ds(pl.multiple_of(lax.rem(number, 2) * 128, 128), 128)

    below, after = (lax.rem(down + 1, n_down), along), (down, lax.rem(along + 1, n_along))
    not_top, not_bottom = down > 0, down < n_down - 1
    not_first, not_last = along > 0, along < n_along - 1

    def exchange(index, source, target, peer):
        copy = remote(source, target, send_sems.at[index], recv_sems.at[index], peer)
        copy.start()
        return copy

    def aligned(start, size):
        return pl.ds(pl.multiple_of(start, 8), size)

    row_copies = [
        exchange(step, grad_probe.at[aligned(peer[1] * part, part)], from_row.at[step], peer) for step, peer in enumerate(row_peers)
    ]
    base = 2 * (n_along + n_down - 2)
    corners, sides, firsts, seconds, hops, forwards = [], [], [], [], [], []
    half = n_down // 2
    wraps, passes = down == half - 1, down == n_down - 1
    over, down_three = (lax.rem(down + half, n_down), along), (lax.rem(down + n_down - 3, n_down), along)
    for layer in range(layers):
        at = base + 4 * layer
        corners.append(remote(rights[layer].at[:, pl.ds(rows, points), :], corner_in.at[layer], send_sems.at[at], recv_sems.at[at], after))
        sides.append(remote(rights[layer].at[:, pl.ds(0, rows), :], right_in.at[layer], send_sems.at[at + 1], recv_sems.at[at + 1], after))
        rest = pl.ds(points, cols - points)
        firsts.append(remote(lowers[layer].at[:, :, rest], lower_in.at[layer, :, :, rest], send_sems.at[at + 2], recv_sems.at[at + 2], below))
        seconds.append(remote(held.at[layer], lower_in.at[layer, :, :, pl.ds(0, points)], send_sems.at[at + 3], recv_sems.at[at + 3], below))
        chunk = points // HOPS
        hops.append([])
        forwards.append([])
        for number in range(HOPS):
            here = pl.ds(number * chunk, chunk)
            hop_at = base + 4 * layers + HOPS * layer + number
            hops[-1].append(remote(
                lowers[layer].at[:, here, rest], relay.at[layer, :, here, :], send_sems.at[hop_at], recv_sems.at[hop_at], over))
            forwards[-1].append(remote(
                relay.at[layer, :, here, :], lower_in.at[layer, :, here, rest], send_sems.at[hop_at], recv_sems.at[at + 2], down_three))
    for layer in range(layers):
        when(not_bottom & not_last, corners[layer].start)

    total = grad_probe[aligned(along * part, part)]
    for step, copy in enumerate(row_copies):
        copy.wait()
        total = total + from_row[step]
    row_sum[...] = total
    at = n_along - 1
    copies = [
        exchange(at + step, row_sum.at[piece_of(peer[0], 0)], from_column.at[step], peer)
        for step, peer in enumerate(column_peers)
    ]
    total = row_sum[piece_of(down, 0)]
    for step, copy in enumerate(copies):
        copy.wait()
        total = total + from_column[step]
    mine = piece_of(down, along * part)
    probe_out[mine] = probe[mine] - scale * total
    at += n_down - 1
    copies = [exchange(at + step, probe_out.at[mine], probe_out.at[mine], peer) for step, peer in enumerate(column_peers)]
    for layer in range(layers):
        for hop in hops[layer]:
            when(wraps, hop.start)
    for layer in range(layers):
        when(not_bottom & ~wraps, firsts[layer].start)
    for copy in copies:
        copy.wait()
    at += n_down - 1
    mine = aligned(along * part, part)
    row_copies = [exchange(at + step, probe_out.at[mine], probe_out.at[mine], peer) for step, peer in enumerate(row_peers)]
    for layer in range(layers):
        when(not_last, sides[layer].start)

    for layer in range(layers):
        loads[layer].wait()
        when(not_bottom & not_first, corners[layer].wait_recv)

        @pl.when(not_bottom & not_first)
        def _():
            held[layer] += corner_in[layer]

        when(not_bottom, seconds[layer].start)
    for layer in range(layers):
        for hop, forward in zip(hops[layer], forwards[layer]):
            when(passes, hop.wait_recv)
            when(passes, forward.start)
    for copy in row_copies:
        copy.wait()
    for layer in range(layers):
        when(not_bottom & not_last, corners[layer].wait_send)
        when(not_last, sides[layer].wait_send)
        when(not_first, sides[layer].wait_recv)
        when(not_bottom & ~wraps, firsts[layer].wait_send)
        when(not_top, firsts[layer].wait_recv)
        for hop, forward in zip(hops[layer], forwards[layer]):
            when(wraps, hop.wait_send)
            when(passes, forward.wait_send)
        when(not_bottom, seconds[layer].wait_send)
        when(not_top, seconds[layer].wait_recv)


def send_back(grad_right, grad_lower, grad_probe, probe_wave, scale, rows):
    layers, _, points, cols = grad_lower.shape
    flat = (2 * points, points)
    n_down, n_along = lax.axis_size("ty"), lax.axis_size("tx")
    part = flat[0] // n_along
    copies = 2 * (n_along + n_down - 2) + (4 + HOPS) * layers
    shape = lambda *dims: jax.ShapeDtypeStruct(dims, jnp.float32)
    right_in, lower_in, probe = pl.pallas_call(
        functools.partial(return_kernel, scale),
        out_shape=[shape(layers, 2, rows, points), shape(layers, 2, points, cols), shape(*flat)],
        in_specs=[ANY, ANY, WHOLE, WHOLE],
        out_specs=[ANY, ANY, WHOLE],
        scratch_shapes=[
            pltpu.VMEM((layers, 2, points, points), jnp.float32),
            pltpu.VMEM((layers, 2, points, points), jnp.float32),
            pltpu.VMEM((layers, 2, points, cols - points), jnp.float32),
            pltpu.VMEM((n_along - 1, part, points), jnp.float32),
            pltpu.VMEM((part, points), jnp.float32),
            pltpu.VMEM((n_down - 1, 8, 128), jnp.float32),
            pltpu.SemaphoreType.DMA((layers,)),
            pltpu.SemaphoreType.DMA((copies,)),
            pltpu.SemaphoreType.DMA((copies,)),
        ],
        compiler_params=pltpu.CompilerParams(collective_id=1, has_side_effects=True, vmem_limit_bytes=VMEM_LIMIT),
    )(grad_right, grad_lower, grad_probe.reshape(flat), probe_wave.reshape(flat))
    return right_in, lower_in, probe.reshape(probe_wave.shape)


def local(object_slab, probe_wave, frames, scan_tiles, scan_offsets):
    columns = lax.axis_size("tx")
    row_index = lax.axis_index("ty")
    col_index = lax.axis_index("tx")
    owned = frames.shape[0]
    points = probe_wave.shape[-1]
    layers, _, tile_rows, tile_cols = object_slab.shape
    total_frames = owned * columns
    my_tile = row_index * columns + col_index
    by_owner = scan_tiles.reshape(columns, owned)

    mine = lax.dynamic_index_in_dim(by_owner, col_index, 0, keepdims=False)
    other_row = lax.rem(row_index + lax.axis_size("ty") // 2, lax.axis_size("ty"))
    places = jnp.arange(columns, dtype=jnp.int32)
    wanted = jnp.concatenate([row_index * columns + places, other_row * columns + places])
    source = jnp.sum((mine[None, :] == wanted[:, None]).astype(jnp.int32) * jnp.arange(owned, dtype=jnp.int32)[None, :], axis=1)

    right, lower, corner, arrived = fetch(source, frames, object_slab, points)

    matches = by_owner == my_tile
    present = jnp.any(matches, axis=1)
    which = jnp.sum(matches.astype(jnp.int32) * jnp.arange(owned, dtype=jnp.int32)[None, :], axis=1)
    global_ids = jnp.arange(columns, dtype=jnp.int32) * owned + which
    ranks = jnp.cumsum(present.astype(jnp.int32)) - 1
    slot_pick = (present[None, :] & (ranks[None, :] == jnp.arange(TILE_CAP, dtype=jnp.int32)[:, None])).astype(jnp.int32)
    chosen_ids = jnp.sum(slot_pick * global_ids[None, :], axis=1)
    owners = jnp.sum(slot_pick * jnp.arange(columns, dtype=jnp.int32)[None, :], axis=1)
    count = jnp.sum(present.astype(jnp.int32)).reshape(1)
    offsets = scan_offsets[chosen_ids].reshape(-1)
    scalars = (offsets, count, owners)

    moved, grad_right, grad_lower, grad_probe = gradients(scalars, object_slab, right, lower, corner, arrived, probe_wave)
    right_back, lower_back, new_probe = send_back(
        grad_right, grad_lower, grad_probe, probe_wave, PROBE_RATE / total_frames, object_slab.shape[2])
    return finish(moved, right_back, lower_back), new_probe


def solution(mesh):
    return jax.shard_map(
        local,
        mesh=mesh,
        in_specs=(P(None, None, "ty", "tx"), P(), P("tx", None, None), P(), P()),
        out_specs=(P(None, None, "ty", "tx"), P()),
        check_vma=False,
    )
```

time: 266 us -> 242 us (0.910)
  the two profiles are of different devices: /device:TPU:104 before, /device:TPU:80 now
where the time goes in v3:
time: 242 us; the launch traced here: 241 us
  Pallas kernels  235 us (97%)
  local copies, waits for them, and re-layouts  3.74 us (2%)
  other arithmetic  2.45 us (1%)
    pallas_call x1, Pallas kernels, send_back(): pl.pallas_call(functools.partial(return_kernel, scale), out_shape=[shape(...  108 us
    pallas_call x1, Pallas kernels, fetch(): pl.pallas_call(fetch_kernel, out_shape=[shape(layers, 2, rows, points), s...  78.4 us
    pallas_call x1, Pallas kernels, gradients(): pl.pallas_call(gradient_kernel, out_shape=[shape(*object_slab.shape), sha...  42 us
    pallas_call x1, Pallas kernels, finish(): pl.pallas_call(finish_kernel, out_shape=jax.ShapeDtypeStruct(moved.shape,...  5.88 us

profile of v3, /device:TPU:80, one launch (start us, length us, event | category | flops | bytes accessed | tf_op | source)
XLA Modules:
  0.0 241.5 jit_solution(17649298773567587627)
XLA Ops:
  0.6 0.1 pad_add_fusion
  0.7 0.8 reshape.76
  1.5 0.1 select_reduce_fusion.1
  1.6 0.7 select_reduce_fusion.source
  2.3 0.1 reduce_or.9
  2.4 0.6 convert_reduce_fusion
  3.0 0.1 copy.14
  3.2 0.1 add_reduce_fusion
  3.3 0.7 select_reduce_fusion.2
  4.0 0.9 copy.15
  4.8 0.6 gather_fusion
  5.4 0.7 reshape.77.offsets
  6.1 78.4 %shard_map.95 = (f32[2,2,512,256]{3,2,1,0:T(8,128)}, f32[2,2,256,512]{3,2,1,0:T(8,128)}, f32[2,2,256,256]{3,2,1,0:T(8,128)}, f32[16,256,256]{2,1,0:T(8,128)}) custom-call(s32[32]{0:T(128)} %select_reduce_fusion.source, f32[48,256,256]{2,1,0:T(8,128)} %frames.1, f32[2,2,512,512]{3,2,1,0:T(8,128)} %slab.3), custom_call_target="tpu_custom_call" | custom-call | tf_op jit(solution)/shard_map/pallas_call | solution.py:492
  84.5 42.0 %shard_map.96 = (f32[2,2,512,512]{3,2,1,0:T(8,128)}, f32[2,2,768,256]{3,2,1,0:T(8,128)}, f32[2,2,256,512]{3,2,1,0:T(8,128)}, f32[2,256,256]{2,1,0:T(8,128)}) custom-call(s32[16]{0:T(128)} %reshape.77.offsets, s32[1]{0:T(128)} %bitcast.3.count, s32[8]{0:T(128)} %get-tuple-element.24.owners, f32[2,2,512,512]{3,2,1,0:T(8,128)} %slab.3, ...), custom_call_target="tpu_custom_call" | custom-call | flops 12884901888 | bytes 33554432 | tf_op jit(solution)/shard_map/pallas_call | solution.py:295
  126.5 108.3 %shard_map.97 = (f32[2,2,512,256]{3,2,1,0:T(8,128)}, f32[2,2,256,512]{3,2,1,0:T(8,128)}, f32[512,256]{1,0:T(8,128)}) custom-call(f32[2,2,768,256]{3,2,1,0:T(8,128)} %get-tuple-element.18.all_right, f32[2,2,256,512]{3,2,1,0:T(8,128)} %get-tuple-element.19.all_lower, f32[512,256]{1,0:T(8,128)} %bitcast.13, f32[512,256]{1,0:T(8,128)} %bitcast.12), custom_call_target="tpu_custom_call" | custom-call | tf_op jit(solution)/shard_map/pallas_call | solution.py:637
  234.8 0.0 copy-start
  234.8 5.9 %shard_map.98 = f32[2,2,512,512]{3,2,1,0:T(8,128)} custom-call(f32[2,2,512,512]{3,2,1,0:T(8,128)} %get-tuple-element.17.moved, f32[2,2,512,256]{3,2,1,0:T(8,128)} %get-tuple-element.21.right, f32[2,2,256,512]{3,2,1,0:T(8,128)} %get-tuple-element.22.lower), custom_call_target="tpu_custom_call" | custom-call | flops 3145728 | bytes 12582912 | tf_op jit(solution)/shard_map/pallas_call | solution.py:334
  240.7 0.0 copy-done
  240.7 0.8 copy.17
  (7 shorter events, 0.1 us)
Async XLA Ops:
  234.8 5.9 %copy-start = (f32[512,256]{1,0:T(8,128)S(1)}, f32[512,256]{1,0:T(8,128)}, u32[]{:S(2)}) copy-start(f32[512,256]{1,0:T(8,128)} %get-tuple-element.23) | copy-start | bytes 1572868

commit v4 on v3

--- a/solution.py
+++ b/solution.py
@@ -358,6 +358,51 @@
     pl.semaphore_wait(barrier, len(peers))
 
 
+def detours(n_down, forward):
+    half = n_down // 2
+    paths = ((half - 1, n_down - 1, half), (half - 1, n_down - 2, half + 1, half), (half - 1, half - 2, half + 1, half))
+    return paths if forward else [tuple(n_down - 1 - place for place in path) for path in paths]
+
+
+def detour(path, along, sources, targets, relay, send_sems, recv_sems, at):
+    hops = len(path) - 1
+    route = []
+    for number, (source, target) in enumerate(zip(sources, targets)):
+        route.append([
+            remote(
+                source if hop == 0 else relay.at[number], target if hop == hops - 1 else relay.at[number],
+                send_sems.at[at + number * hops + hop], recv_sems.at[at + number * hops + hop], (jnp.int32(path[hop + 1]), along))
+            for hop in range(hops)
+        ])
+    return route
+
+
+def set_off(route, path, down):
+    for copies in route:
+        when(down == path[0], copies[0].start)
+
+
+def pass_on(routes, paths, down):
+    for number in range(len(routes[0])):
+        for route, path in zip(routes, paths):
+            for hop in range(1, len(path) - 1):
+                when(down == path[hop], route[number][hop - 1].wait_recv)
+                when(down == path[hop], route[number][hop].start)
+
+
+def arrive(routes, paths, down):
+    for route, path in zip(routes, paths):
+        for copies in route:
+            when(down == path[-1], copies[-1].wait_recv)
+
+
+def settle(routes, paths, down):
+    for route, path in zip(routes, paths):
+        for copies in route:
+            for hop, copy in enumerate(copies):
+                when(down == path[hop], copy.wait_send)
+
+
 def around(down, along, n_down, n_along):
     row = [(down, lax.rem(along + step, n_along)) for step in range(1, n_along)]
     column = [(lax.rem(down + step, n_down), along) for step in range(1, n_down)]
@@ -390,7 +435,8 @@
     above, left = ring(-1, 0), ring(0, -1)
     not_top, not_bottom = down > 0, down < n_down - 1
     not_first, not_last = along > 0, along < n_along - 1
-    wraps, passes = down == half, down == 0
+    paths = detours(n_down, False)
+    wraps, joins = down == half, down == half - 1
     crosses, carries = lax.rem(along, 4) == 0, lax.rem(along, 4) == 3
     crossed = carries & not_last
     across = crosses & not_first
@@ -405,30 +451,31 @@
     side = [slab.at[layer, :, :, pl.ds(0, points)] for layer in range(layers)]
     edge = [lower.at[layer, :, :, pl.ds(0, points)] for layer in range(layers)]
     rest, start = pl.ds(points, cols - points), pl.ds(0, points)
-    lowers, others, hops, forwards, rights, corners = [], [], [], [], [], []
+    lowers, others, rights, corners = [], [], [], []
     for layer in range(layers):
         lowers.append(copy(slab.at[layer, :, pl.ds(0, points), start], lower.at[layer, :, :, start], above))
-        at = next(index)
-        others.append(copy(slab.at[layer, :, pl.ds(0, points), rest], lower.at[layer, :, :, rest], above, at))
-        chunk = points // HOPS
-        for number in range(HOPS):
-            here = pl.ds(number * chunk, chunk)
-            hop_at = next(index)
-            hops.append(copy(slab.at[layer, :, here, rest], lower_relay.at[layer, :, here, :], ring(half, 0), hop_at))
-            forwards.append(remote(
-                lower_relay.at[layer, :, here, :], lower.at[layer, :, here, rest], send_sems.at[hop_at], recv_sems.at[at], ring(3, 0)))
+        others.append(copy(slab.at[layer, :, pl.ds(0, points), rest], lower.at[layer, :, :, rest], above))
         rights.append(copy(side[layer], right.at[layer], left))
         corners.append(copy(edge[layer], corner.at[layer], left))
-    per_layer = 4 + HOPS
-    at_right, at_corner = base + per_layer * layers - 2, base + per_layer * layers - 1
+    at_right, at_corner = base + 4 * last + 2, base + 4 * last + 3
     right_hop = copy(side[last], right_relay.at[:, pl.ds(0, rows), :], ring(0, 3))
     right_forward = copy(right_relay.at[:, pl.ds(0, rows), :], right.at[last], ring(0, -4), at_right)
     corner_hop = copy(edge[last], right_relay.at[:, pl.ds(rows, points), :], ring(0, 3))
     corner_forward = copy(right_relay.at[:, pl.ds(rows, points), :], corner.at[last], ring(0, -4), at_corner)
 
-    for layer in range(layers):
-        when(not_top, lowers[layer].start)
-        when(not_top & ~wraps, others[layer].start)
+    chunk = points // HOPS
+    routes = []
+    at = base + 4 * layers + 2
+    for number, (path, layer, lanes) in enumerate(zip(paths, (last, first, last), (start, rest, rest))):
+        pieces = [pl.ds(piece * chunk, chunk) for piece in range(HOPS)]
+        routes.append(detour(
+            path, along, [slab.at[layer, :, piece, lanes] for piece in pieces], [lower.at[layer, :, piece, lanes] for piece in pieces],
+            lower_relay.at[number], send_sems, recv_sems, at))
+        at += HOPS * (len(path) - 1)
+    ahead = (lowers[first], lowers[last], others[first], others[last])
+    when(not_top, lowers[first].start)
+    for go in ahead[1:]:
+        when(not_top & ~wraps, go.start)
     when(across, right_hop.start)
     when(not_first & ~crosses, rights[last].start)
     when(not_first, rights[first].start)
@@ -440,19 +487,21 @@
         send = remote(picked.at[step], arrived.at[along], send_sems.at[step], recv_sems.at[step], peer)
         send.start()
         sends.append(send)
-    for hop in hops:
-        when(wraps, hop.start)
+    for route, path in zip(routes, paths):
+        set_off(route, path, down)
     picked[n_along - 1] = held[source[along]]
     own = pltpu.make_async_copy(picked.at[n_along - 1], arrived.at[along], own_sem)
     own.start()
     relays = along >= 4
-    for hop, forward in zip(hops, forwards):
-        when(passes, hop.wait_recv)
-        when(passes, forward.start)
     when(carries & relays, right_hop.wait_recv)
     when(carries & relays, right_forward.start)
-    for layer in range(layers):
-        when(not_bottom, lowers[layer].wait_recv)
+    pass_on(routes, paths, down)
+    for layer in range(layers):
+        if layer == last:
+            arrive(routes[:1], paths[:1], down)
+            when(not_bottom & ~joins, lowers[layer].wait_recv)
+        else:
+            when(not_bottom, lowers[layer].wait_recv)
         if layer == last:
             when(not_bottom & across, corner_hop.start)
             when(not_bottom & not_first & ~crosses, corners[layer].start)
@@ -460,12 +509,13 @@
             when(not_bottom & carries & relays, corner_forward.start)
         else:
             when(not_bottom & not_first, corners[layer].start)
-    for layer in range(layers):
-        when(not_bottom, others[layer].wait_recv)
+    when(not_top, lowers[first].wait_send)
+    for go in ahead[1:]:
+        when(not_top & ~wraps, go.wait_send)
+    for layer in range(layers):
+        when(not_bottom & ~joins, others[layer].wait_recv)
         when(not_last, rights[layer].wait_recv)
         when(not_bottom & not_last, corners[layer].wait_recv)
-        when(not_top, lowers[layer].wait_send)
-        when(not_top & ~wraps, others[layer].wait_send)
         if layer == last:
             when(across, right_hop.wait_send)
             when(not_first & ~crosses, rights[layer].wait_send)
@@ -476,9 +526,8 @@
         else:
             when(not_first, rights[layer].wait_send)
             when(not_bottom & not_first, corners[layer].wait_send)
-    for hop, forward in zip(hops, forwards):
-        when(wraps, hop.wait_send)
-        when(passes, forward.wait_send)
+    arrive(routes[1:], paths[1:], down)
+    settle(routes, paths, down)
     for send in sends:
         send.wait()
     own.wait()
@@ -487,7 +536,7 @@
 def fetch(source, frames, object_slab, points):
     layers, _, rows, cols = object_slab.shape
     n_along = lax.axis_size("tx")
-    copies = n_along - 1 + (4 + HOPS) * layers + 2
+    copies = n_along - 1 + 4 * layers + 2 + 8 * HOPS
     shape = lambda *dims: jax.ShapeDtypeStruct(dims, jnp.float32)
     return pl.pallas_call(
         fetch_kernel,
@@ -498,7 +547,7 @@
         scratch_shapes=[
             pltpu.VMEM(frames.shape, jnp.float32),
             pltpu.VMEM((n_along, points, points), jnp.float32),
-            pltpu.VMEM((layers, 2, points, cols - points), jnp.float32),
+            pltpu.VMEM((3, HOPS, 2, points // HOPS, points), jnp.float32),
             pltpu.VMEM((2, rows + points, points), jnp.float32),
             pltpu.SemaphoreType.DMA,
             pltpu.SemaphoreType.DMA,
@@ -544,30 +593,34 @@
         exchange(step, grad_probe.at[aligned(peer[1] * part, part)], from_row.at[step], peer) for step, peer in enumerate(row_peers)
     ]
     base = 2 * (n_along + n_down - 2)
-    corners, sides, firsts, seconds, hops, forwards = [], [], [], [], [], []
+    corners, sides, firsts, seconds = [], [], [], []
     half = n_down // 2
-    wraps, passes = down == half - 1, down == n_down - 1
-    over, down_three = (lax.rem(down + half, n_down), along), (lax.rem(down + n_down - 3, n_down), along)
+    paths = detours(n_down, True)
+    wraps, joins = down == half - 1, down == half
+    start, rest = pl.ds(0, points), pl.ds(points, cols - points)
     for layer in range(layers):
         at = base + 4 * layer
         corners.append(remote(rights[layer].at[:, pl.ds(rows, points), :], corner_in.at[layer], send_sems.at[at], recv_sems.at[at], after))
         sides.append(remote(rights[layer].at[:, pl.ds(0, rows), :], right_in.at[layer], send_sems.at[at + 1], recv_sems.at[at + 1], after))
-        rest = pl.ds(points, cols - points)
         firsts.append(remote(lowers[layer].at[:, :, rest], lower_in.at[layer, :, :, rest], send_sems.at[at + 2], recv_sems.at[at + 2], below))
-        seconds.append(remote(held.at[layer], lower_in.at[layer, :, :, pl.ds(0, points)], send_sems.at[at + 3], recv_sems.at[at + 3], below))
-        chunk = points // HOPS
-        hops.append([])
-        forwards.append([])
-        for number in range(HOPS):
-            here = pl.ds(number * chunk, chunk)
-            hop_at = base + 4 * layers + HOPS * layer + number
-            hops[-1].append(remote(
-                lowers[layer].at[:, here, rest], relay.at[layer, :, here, :], send_sems.at[hop_at], recv_sems.at[hop_at], over))
-            forwards[-1].append(remote(
-                relay.at[layer, :, here, :], lower_in.at[layer, :, here, rest], send_sems.at[hop_at], recv_sems.at[at + 2], down_three))
+        seconds.append(remote(held.at[layer], lower_in.at[layer, :, :, start], send_sems.at[at + 3], recv_sems.at[at + 3], below))
+    first, last = 0, layers - 1
+    chunk = points // HOPS
+    pieces = [pl.ds(piece * chunk, chunk) for piece in range(HOPS)]
+    routes = []
+    at = base + 4 * layers
+    for number, (path, layer) in enumerate(zip(paths, (last, first, last))):
+        if number == 0:
+            sources, lanes = [held.at[layer, :, piece, :] for piece in pieces], start
+        else:
+            sources, lanes = [lowers[layer].at[:, piece, rest] for piece in pieces], rest
+        routes.append(detour(
+            path, along, sources, [lower_in.at[layer, :, piece, lanes] for piece in pieces], relay.at[number], send_sems, recv_sems, at))
+        at += HOPS * (len(path) - 1)
     for layer in range(layers):
         when(not_bottom & not_last, corners[layer].start)
 
+    when(not_bottom & ~wraps, firsts[0].start)
     total = grad_probe[aligned(along * part, part)]
     for step, copy in enumerate(row_copies):
         copy.wait()
@@ -586,16 +639,15 @@
     probe_out[mine] = probe[mine] - scale * total
     at += n_down - 1
     copies = [exchange(at + step, probe_out.at[mine], probe_out.at[mine], peer) for step, peer in enumerate(column_peers)]
-    for layer in range(layers):
-        for hop in hops[layer]:
-            when(wraps, hop.start)
-    for layer in range(layers):
+    for layer in range(1, layers):
         when(not_bottom & ~wraps, firsts[layer].start)
     for copy in copies:
         copy.wait()
     at += n_down - 1
     mine = aligned(along * part, part)
     row_copies = [exchange(at + step, probe_out.at[mine], probe_out.at[mine], peer) for step, peer in enumerate(row_peers)]
+    for route, path in zip(routes[1:], paths[1:]):
+        set_off(route, path, down)
     for layer in range(layers):
         when(not_last, sides[layer].start)
 
@@ -607,11 +659,13 @@
         def _():
             held[layer] += corner_in[layer]
 
-        when(not_bottom, seconds[layer].start)
-    for layer in range(layers):
-        for hop, forward in zip(hops[layer], forwards[layer]):
-            when(passes, hop.wait_recv)
-            when(passes, forward.start)
+        if layer == last:
+            set_off(routes[0], paths[0], down)
+            when(not_bottom & ~wraps, seconds[layer].start)
+        else:
+            when(not_bottom, seconds[layer].start)
+    pass_on(routes[1:], paths[1:], down)
+    pass_on(routes[:1], paths[:1], down)
     for copy in row_copies:
         copy.wait()
     for layer in range(layers):
@@ -619,12 +673,15 @@
         when(not_last, sides[layer].wait_send)
         when(not_first, sides[layer].wait_recv)
         when(not_bottom & ~wraps, firsts[layer].wait_send)
-        when(not_top, firsts[layer].wait_recv)
-        for hop, forward in zip(hops[layer], forwards[layer]):
-            when(wraps, hop.wait_send)
-            when(passes, forward.wait_send)
-        when(not_bottom, seconds[layer].wait_send)
-        when(not_top, seconds[layer].wait_recv)
+        when(not_top & ~joins, firsts[layer].wait_recv)
+        if layer == last:
+            when(not_bottom & ~wraps, seconds[layer].wait_send)
+            when(not_top & ~joins, seconds[layer].wait_recv)
+        else:
+            when(not_bottom, seconds[layer].wait_send)
+            when(not_top, seconds[layer].wait_recv)
+    arrive(routes, paths, down)
+    settle(routes, paths, down)
 
 
 def send_back(grad_right, grad_lower, grad_probe, probe_wave, scale, rows):
@@ -632,7 +689,7 @@
     flat = (2 * points, points)
     n_down, n_along = lax.axis_size("ty"), lax.axis_size("tx")
     part = flat[0] // n_along
-    copies = 2 * (n_along + n_down - 2) + (4 + HOPS) * layers
+    copies = 2 * (n_along + n_down - 2) + 4 * layers + 8 * HOPS
     shape = lambda *dims: jax.ShapeDtypeStruct(dims, jnp.float32)
     right_in, lower_in, probe = pl.pallas_call(
         functools.partial(return_kernel, scale),
@@ -642,7 +699,7 @@
         scratch_shapes=[
             pltpu.VMEM((layers, 2, points, points), jnp.float32),
             pltpu.VMEM((layers, 2, points, points), jnp.float32),
-            pltpu.VMEM((layers, 2, points, cols - points), jnp.float32),
+            pltpu.VMEM((3, HOPS, 2, points // HOPS, points), jnp.float32),
             pltpu.VMEM((n_along - 1, part, points), jnp.float32),
             pltpu.VMEM((part, points), jnp.float32),
             pltpu.VMEM((n_down - 1, 8, 128), jnp.float32),

time: 242 us -> 217 us (0.90)
  the two profiles are of different devices: /device:TPU:80 before, /device:TPU:104 now
where the time goes in v4:
time: 217 us
  Pallas kernels  210 us (97%)
  local copies, waits for them, and re-layouts  3.74 us (2%)
  other arithmetic  2.45 us (1%)
    pallas_call x1, Pallas kernels, send_back(): pl.pallas_call(functools.partial(return_kernel, scale), out_shape=[shape(...  91 us
    pallas_call x1, Pallas kernels, fetch(): pl.pallas_call(fetch_kernel, out_shape=[shape(layers, 2, rows, points), s...  70.8 us
    pallas_call x1, Pallas kernels, gradients(): pl.pallas_call(gradient_kernel, out_shape=[shape(*object_slab.shape), sha...  42.1 us
    pallas_call x1, Pallas kernels, finish(): pl.pallas_call(finish_kernel, out_shape=jax.ShapeDtypeStruct(moved.shape,...  5.88 us

profile of v4, /device:TPU:104, one launch (start us, length us, event | category | flops | bytes accessed | tf_op | source)
XLA Modules:
  0.0 216.6 jit_solution(17719221416940253655)
XLA Ops:
  0.6 0.1 pad_add_fusion
  0.7 0.8 reshape.76
  1.5 0.1 select_reduce_fusion.1
  1.6 0.7 select_reduce_fusion.source
  2.3 0.1 reduce_or.9
  2.4 0.6 convert_reduce_fusion
  3.0 0.1 copy.14
  3.2 0.1 add_reduce_fusion
  3.3 0.7 select_reduce_fusion.2
  4.0 0.9 copy.15
  4.8 0.6 gather_fusion
  5.4 0.7 reshape.77.offsets
  6.1 70.8 %shard_map.95 = (f32[2,2,512,256]{3,2,1,0:T(8,128)}, f32[2,2,256,512]{3,2,1,0:T(8,128)}, f32[2,2,256,256]{3,2,1,0:T(8,128)}, f32[16,256,256]{2,1,0:T(8,128)}) custom-call(s32[32]{0:T(128)} %select_reduce_fusion.source, f32[48,256,256]{2,1,0:T(8,128)} %frames.1, f32[2,2,512,512]{3,2,1,0:T(8,128)} %slab.3), custom_call_target="tpu_custom_call" | custom-call | tf_op jit(solution)/shard_map/pallas_call | solution.py:541
  76.8 42.1 %shard_map.96 = (f32[2,2,512,512]{3,2,1,0:T(8,128)}, f32[2,2,768,256]{3,2,1,0:T(8,128)}, f32[2,2,256,512]{3,2,1,0:T(8,128)}, f32[2,256,256]{2,1,0:T(8,128)}) custom-call(s32[16]{0:T(128)} %reshape.77.offsets, s32[1]{0:T(128)} %bitcast.3.count, s32[8]{0:T(128)} %get-tuple-element.24.owners, f32[2,2,512,512]{3,2,1,0:T(8,128)} %slab.3, ...), custom_call_target="tpu_custom_call" | custom-call | flops 12884901888 | bytes 33554432 | tf_op jit(solution)/shard_map/pallas_call | solution.py:295
  118.9 91.0 %shard_map.97 = (f32[2,2,512,256]{3,2,1,0:T(8,128)}, f32[2,2,256,512]{3,2,1,0:T(8,128)}, f32[512,256]{1,0:T(8,128)}) custom-call(f32[2,2,768,256]{3,2,1,0:T(8,128)} %get-tuple-element.18.all_right, f32[2,2,256,512]{3,2,1,0:T(8,128)} %get-tuple-element.19.all_lower, f32[512,256]{1,0:T(8,128)} %bitcast.13, f32[512,256]{1,0:T(8,128)} %bitcast.12), custom_call_target="tpu_custom_call" | custom-call | tf_op jit(solution)/shard_map/pallas_call | solution.py:694
  209.9 0.0 copy-start
  209.9 5.9 %shard_map.98 = f32[2,2,512,512]{3,2,1,0:T(8,128)} custom-call(f32[2,2,512,512]{3,2,1,0:T(8,128)} %get-tuple-element.17.moved, f32[2,2,512,256]{3,2,1,0:T(8,128)} %get-tuple-element.21.right, f32[2,2,256,512]{3,2,1,0:T(8,128)} %get-tuple-element.22.lower), custom_call_target="tpu_custom_call" | custom-call | flops 3145728 | bytes 12582912 | tf_op jit(solution)/shard_map/pallas_call | solution.py:334
  215.8 0.0 copy-done
  215.8 0.8 copy.17
  (7 shorter events, 0.1 us)
Async XLA Ops:
  209.9 5.9 %copy-start = (f32[512,256]{1,0:T(8,128)S(1)}, f32[512,256]{1,0:T(8,128)}, u32[]{:S(2)}) copy-start(f32[512,256]{1,0:T(8,128)} %get-tuple-element.23) | copy-start | bytes 1572868

commit v5 on v4

--- a/solution.py
+++ b/solution.py
@@ -13,6 +13,8 @@
 MESH = pl.DeviceIdType.MESH
 TILE_CAP = 8
 HOPS = 4
+PAIR = 2
+EARLY_FRAMES = (12, 14)
 BACKGROUND = 0.5
 FRESNEL = 0.25
 OBJECT_RATE = 0.25
@@ -36,10 +38,6 @@
 
 def left_table(table):
     return np.concatenate(split_table(table), axis=1)
-
-
-def right_table(table):
-    return np.concatenate(split_table(table), axis=0)
 
 
 def half_transforms(points):
@@ -63,9 +61,7 @@
     shuffle = (places[:, None] == order[None, :]).astype(ml_dtypes.bfloat16)
 
     groups = [spread, [table.T for table in spread], fourier, [table.T for table in fourier]]
-    left = np.stack([left_table(table) for group in groups for table in group])
-    right = np.stack([right_table(table.T) for group in groups for table in group])
-    return left, right, shuffle
+    return np.stack([left_table(table) for group in groups for table in group]), shuffle
 
 
 def split(value):
@@ -84,7 +80,7 @@
 def right_product(value, table):
     high, low = split(value)
     size = value.shape[1]
-    table = jnp.concatenate([table[...], table[:size, :]], axis=0)
+    table = jnp.concatenate([table[:, :size], table[:, size:], table[:, :size]], axis=0)
     return jnp.dot(jnp.concatenate([high, high, low], axis=1), table, preferred_element_type=jnp.float32)
 
 
@@ -176,15 +172,15 @@
     return a[0] * b[0] + a[1] * b[1], a[0] * b[1] - a[1] * b[0]
 
 
-def gradient_kernel(offsets, count, owners, slab, right, lower, corner, arrived, probe, left_all, right_all, shuffle_all, moved,
-                    grad_right, grad_lower, grad_probe, canvas, grad, frame, columns, left_held, right_held, shuffle, load_sems,
+def gradient_kernel(row_offsets, column_offsets, count, owners, slab, right, lower, corner, arrived, probe, tables_all, shuffle_all, moved,
+                    grad_right, grad_lower, grad_probe, canvas, grad, frame, columns, tables, shuffle, load_sems,
                     table_sems, frame_sems, out_sems):
     table_loads = [
         pltpu.make_async_copy(source, target, table_sems.at[at])
-        for at, (source, target) in enumerate(((left_all, left_held), (right_all, right_held), (shuffle_all, shuffle)))
+        for at, (source, target) in enumerate(((tables_all, tables), (shuffle_all, shuffle)))
     ]
     spread_ahead, spread_back, fourier_ahead, fourier_back = (
-        [left_held.at[at], left_held.at[at + 1], right_held.at[at], right_held.at[at + 1]] for at in range(0, 8, 2))
+        [tables.at[at] for at in order] for order in ((0, 1, 2, 3), (2, 3, 0, 1), (4, 5, 6, 7), (6, 7, 4, 5)))
     layers, rows, cols = slab.shape[0], slab.shape[2], slab.shape[3]
     points = probe.shape[1]
     half = points // 2
@@ -194,24 +190,31 @@
     def lanes(number):
         return pl.ds(128 * number, 128)
 
-    def frame_copy(slot):
-        return pltpu.make_async_copy(arrived.at[owners[slot]], frame.at[lax.rem(slot, 2)], frame_sems.at[lax.rem(slot, 2)])
-
-    pairs = []
+    pairs = (count[0] + PAIR - 1) // PAIR
+
+    def frame_copies(pair):
+        side = lax.rem(pair, 2)
+        return [
+            pltpu.make_async_copy(arrived.at[owners[PAIR * pair + at]], frame.at[side, at], frame_sems.at[side, at])
+            for at in range(PAIR)
+        ]
+
+    parts = []
     for layer in range(layers):
         for number in range(own_lanes):
-            pairs.append((slab.at[layer, :, :, lanes(number)], canvas.at[layer, :, number, own, :]))
-            pairs.append((lower.at[layer, :, :, lanes(number)], canvas.at[layer, :, number, beside, :]))
+            parts.append((slab.at[layer, :, :, lanes(number)], canvas.at[layer, :, number, own, :]))
+            parts.append((lower.at[layer, :, :, lanes(number)], canvas.at[layer, :, number, beside, :]))
         for number in range(more_lanes):
-            pairs.append((right.at[layer, :, :, lanes(number)], canvas.at[layer, :, own_lanes + number, own, :]))
-            pairs.append((corner.at[layer, :, :, lanes(number)], canvas.at[layer, :, own_lanes + number, beside, :]))
-    loads = [pltpu.make_async_copy(source, target, load_sems.at[at]) for at, (source, target) in enumerate(pairs)]
+            parts.append((right.at[layer, :, :, lanes(number)], canvas.at[layer, :, own_lanes + number, own, :]))
+            parts.append((corner.at[layer, :, :, lanes(number)], canvas.at[layer, :, own_lanes + number, beside, :]))
+    loads = [pltpu.make_async_copy(source, target, load_sems.at[at]) for at, (source, target) in enumerate(parts)]
     for load in loads + table_loads:
         load.start()
 
     @pl.when(count[0] > 0)
     def _():
-        frame_copy(0).start()
+        for copy in frame_copies(0):
+            copy.start()
 
     grad[...] = jnp.zeros_like(grad)
     grad_probe[...] = jnp.zeros_like(grad_probe)
@@ -226,42 +229,50 @@
     def _():
         canvas[:, :, pl.ds(own_lanes, more_lanes)] = jnp.zeros((layers, 2, more_lanes, rows + points, 128), jnp.float32)
 
-    def visit(slot, carry):
-        place = place_of(offsets[2 * slot], offsets[2 * slot + 1], points)
-        frame_copy(slot).wait()
-
-        @pl.when(slot + 1 < count[0])
+    def visit(pair, carry):
+        slots = [PAIR * pair + at for at in range(PAIR)]
+        places = [place_of(row_offsets[slot], column_offsets[slot], points) for slot in slots]
+        for copy in frame_copies(pair):
+            copy.wait()
+
+        @pl.when(pair + 1 < pairs)
         def _():
-            frame_copy(slot + 1).start()
+            for copy in frame_copies(pair + 1):
+                copy.start()
 
         probe_wave = (probe[0], probe[1])
-        windows = [window_of(canvas, layer, place, points) for layer in range(layers)]
-        wave = spread(*times(probe_wave, windows[0]), spread_ahead)
-        real, imag = to_frequencies(*times(wave, windows[1]), fourier_ahead)
-        pieces = []
-        for side in range(points // 128):
-            columns[side] = jnp.sqrt(frame[lax.rem(slot, 2), :, pl.ds(side * 128, 128)] + BACKGROUND)
-            pieces.append(jnp.concatenate([columns[side, pl.ds(start, half, stride=2), :] for start in range(2)], axis=0))
-        target = jnp.concatenate(pieces, axis=1)
-        high = target.astype(jnp.bfloat16)
-        rest = target - high.astype(jnp.float32)
-        middle = rest.astype(jnp.bfloat16)
-        low = (rest - middle.astype(jnp.float32)).astype(jnp.bfloat16)
-        target = jnp.dot(
-            jnp.concatenate([high, middle, low], axis=1), jnp.concatenate([shuffle[...]] * 3, axis=0),
-            preferred_element_type=jnp.float32)
-        pull = 2.0 - 2.0 * target * lax.rsqrt(real * real + imag * imag + BACKGROUND)
-        back = from_frequencies(pull * real, pull * imag, fourier_back)
-        add_window(grad, 1, place, points, times_conjugate(wave, back))
-        back = times_conjugate(windows[1], back)
-        back = spread(*back, spread_back)
-        add_window(grad, 0, place, points, times_conjugate(probe_wave, back))
-        more = times_conjugate(windows[0], back)
-        grad_probe[0] += more[0]
-        grad_probe[1] += more[1]
+        windows = [[window_of(canvas, layer, place, points) for layer in range(layers)] for place in places]
+        waves = [spread(*times(probe_wave, window[0]), spread_ahead) for window in windows]
+        fars = [to_frequencies(*times(wave, window[1]), fourier_ahead) for wave, window in zip(waves, windows)]
+        backs = []
+        for at, (real, imag) in enumerate(fars):
+            pieces = []
+            for side in range(points // 128):
+                columns[at, side] = jnp.sqrt(frame[lax.rem(pair, 2), at, :, pl.ds(side * 128, 128)] + BACKGROUND)
+                pieces.append(jnp.concatenate([columns[at, side, pl.ds(start, half, stride=2), :] for start in range(2)], axis=0))
+            target = jnp.concatenate(pieces, axis=1)
+            high = target.astype(jnp.bfloat16)
+            rest = target - high.astype(jnp.float32)
+            middle = rest.astype(jnp.bfloat16)
+            low = (rest - middle.astype(jnp.float32)).astype(jnp.bfloat16)
+            target = jnp.dot(
+                jnp.concatenate([high, middle, low], axis=1), jnp.concatenate([shuffle[...]] * 3, axis=0),
+                preferred_element_type=jnp.float32)
+            pull = 2.0 - 2.0 * target * lax.rsqrt(real * real + imag * imag + BACKGROUND)
+            pull = pull * (slots[at] < count[0]).astype(jnp.float32)
+            backs.append((pull * real, pull * imag))
+        backs = [from_frequencies(*back, fourier_back) for back in backs]
+        for place, wave, back in zip(places, waves, backs):
+            add_window(grad, 1, place, points, times_conjugate(wave, back))
+        backs = [spread(*times_conjugate(window[1], back), spread_back) for window, back in zip(windows, backs)]
+        for place, back in zip(places, backs):
+            add_window(grad, 0, place, points, times_conjugate(probe_wave, back))
+        more = [times_conjugate(window[0], back) for window, back in zip(windows, backs)]
+        for part in range(2):
+            grad_probe[part] += sum(one[part] for one in more)
         return carry
 
-    lax.fori_loop(0, count[0], visit, 0)
+    lax.fori_loop(0, pairs, visit, 0)
     writes = [
         pltpu.make_async_copy(grad.at[:, :, own_lanes + number], grad_right.at[:, :, :, lanes(number)], out_sems.at[number])
         for number in range(more_lanes)
@@ -303,12 +314,12 @@
             out_specs=[ANY] * 3 + [WHOLE],
             scratch_shapes=[
                 canvas, canvas,
-                pltpu.VMEM((2, points, points), jnp.float32),
-                pltpu.VMEM((points // 128, points, 128), jnp.float32),
+                pltpu.VMEM((2, PAIR, points, points), jnp.float32),
+                pltpu.VMEM((PAIR, points // 128, points, 128), jnp.float32),
                 *[pltpu.VMEM(table.shape, jnp.bfloat16) for table in tables],
                 pltpu.SemaphoreType.DMA((2 * layers * lanes,)),
                 pltpu.SemaphoreType.DMA((len(tables),)),
-                pltpu.SemaphoreType.DMA((2,)),
+                pltpu.SemaphoreType.DMA((2, PAIR)),
                 pltpu.SemaphoreType.DMA((lanes + cols // 128,)),
             ]),
         compiler_params=pltpu.CompilerParams(vmem_limit_bytes=VMEM_LIMIT),
@@ -481,12 +492,16 @@
     when(not_first, rights[first].start)
     load.wait()
     sends = []
-    for step, offset in enumerate(FRAME_STEPS):
-        peer, other = frame_peer(down, along, n_down, n_along, offset, True)
-        picked[step] = held[source[other * n_along + peer[1]]]
-        send = remote(picked.at[step], arrived.at[along], send_sems.at[step], recv_sems.at[step], peer)
-        send.start()
-        sends.append(send)
+
+    def send_frames(steps):
+        for step in steps:
+            peer, other = frame_peer(down, along, n_down, n_along, FRAME_STEPS[step], True)
+            picked[step] = held[source[other * n_along + peer[1]]]
+            send = remote(picked.at[step], arrived.at[along], send_sems.at[step], recv_sems.at[step], peer)
+            send.start()
+            sends.append(send)
+
+    send_frames(range(EARLY_FRAMES[0]))
     for route, path in zip(routes, paths):
         set_off(route, path, down)
     picked[n_along - 1] = held[source[along]]
@@ -509,6 +524,8 @@
             when(not_bottom & carries & relays, corner_forward.start)
         else:
             when(not_bottom & not_first, corners[layer].start)
+            send_frames(range(EARLY_FRAMES[0], EARLY_FRAMES[1]))
+    send_frames(range(EARLY_FRAMES[1], len(FRAME_STEPS)))
     when(not_top, lowers[first].wait_send)
     for go in ahead[1:]:
         when(not_top & ~wraps, go.wait_send)
@@ -731,17 +748,15 @@
 
     right, lower, corner, arrived = fetch(source, frames, object_slab, points)
 
-    matches = by_owner == my_tile
-    present = jnp.any(matches, axis=1)
-    which = jnp.sum(matches.astype(jnp.int32) * jnp.arange(owned, dtype=jnp.int32)[None, :], axis=1)
-    global_ids = jnp.arange(columns, dtype=jnp.int32) * owned + which
-    ranks = jnp.cumsum(present.astype(jnp.int32)) - 1
-    slot_pick = (present[None, :] & (ranks[None, :] == jnp.arange(TILE_CAP, dtype=jnp.int32)[:, None])).astype(jnp.int32)
-    chosen_ids = jnp.sum(slot_pick * global_ids[None, :], axis=1)
-    owners = jnp.sum(slot_pick * jnp.arange(columns, dtype=jnp.int32)[None, :], axis=1)
-    count = jnp.sum(present.astype(jnp.int32)).reshape(1)
-    offsets = scan_offsets[chosen_ids].reshape(-1)
-    scalars = (offsets, count, owners)
+    matches = (by_owner == my_tile).astype(jnp.int32)
+    present = jnp.sum(matches, axis=1)
+    ranks = jnp.cumsum(present) - 1
+    slot_pick = present[None, :] * (ranks[None, :] == jnp.arange(TILE_CAP, dtype=jnp.int32)[:, None]).astype(jnp.int32)
+    by_slot = lambda values: jnp.sum(slot_pick * values[None, :], axis=1)
+    row_offsets, column_offsets = (
+        by_slot(jnp.sum(matches * scan_offsets[:, side].reshape(columns, owned), axis=1)) for side in range(2))
+    owners = by_slot(places)
+    scalars = (row_offsets, column_offsets, jnp.sum(present).reshape(1), owners)
 
     moved, grad_right, grad_lower, grad_probe = gradients(scalars, object_slab, right, lower, corner, arrived, probe_wave)
     right_back, lower_back, new_probe = send_back(

time: 217 us -> 209 us (0.963)
  Pallas kernels: 210 us -> 202 us
    pallas_call x1, Pallas kernels: 42.1 us -> 35.2 us  [gradients(): pl.pallas_call(gradient_kernel, out_shape=[shape(*object_slab.shape), sha...]
    pallas_call x1, Pallas kernels: 91 us -> 84.7 us  [send_back(): pl.pallas_call(functools.partial(return_kernel, scale), out_shape=[shape(...]
    pallas_call x1, Pallas kernels: 70.8 us -> 76.3 us  [fetch(): pl.pallas_call(fetch_kernel, out_shape=[shape(layers, 2, rows, points), s...]
where the time goes in v5:
time: 209 us; the launch traced here: 208 us
  Pallas kernels  202 us (97%)
  other arithmetic  3.15 us (2%)
  local copies, waits for them, and re-layouts  2.58 us (1%)
    pallas_call x1, Pallas kernels, send_back(): pl.pallas_call(functools.partial(return_kernel, scale), out_shape=[shape(...  84.7 us
    pallas_call x1, Pallas kernels, fetch(): pl.pallas_call(fetch_kernel, out_shape=[shape(layers, 2, rows, points), s...  76.3 us
    pallas_call x1, Pallas kernels, gradients(): pl.pallas_call(gradient_kernel, out_shape=[shape(*object_slab.shape), sha...  35.2 us
    pallas_call x1, Pallas kernels, finish(): pl.pallas_call(finish_kernel, out_shape=jax.ShapeDtypeStruct(moved.shape,...  5.88 us

profile of v5, /device:TPU:104, one launch (start us, length us, event | category | flops | bytes accessed | tf_op | source)
XLA Modules:
  0.0 208.5 jit_solution(9254725490409397742)
XLA Ops:
  0.6 1.3 convert_reduce_fusion.1
  2.0 0.1 pad_add_fusion
  2.1 0.8 reshape.58
  2.8 0.7 select_reduce_fusion.source
  3.5 0.8 slice_reduce_fusion
  4.3 0.1 reshape_squeeze.7
  4.4 0.1 reshape_squeeze.6
  4.5 0.2 select_reduce_fusion.1
  4.6 0.1 copy.11
  4.7 0.1 add_reduce_fusion
  4.9 0.7 fusion.2
  5.6 76.3 %shard_map.86 = (f32[2,2,512,256]{3,2,1,0:T(8,128)}, f32[2,2,256,512]{3,2,1,0:T(8,128)}, f32[2,2,256,256]{3,2,1,0:T(8,128)}, f32[16,256,256]{2,1,0:T(8,128)}) custom-call(s32[32]{0:T(128)} %select_reduce_fusion.source, f32[48,256,256]{2,1,0:T(8,128)} %frames.1, f32[2,2,512,512]{3,2,1,0:T(8,128)} %slab.3), custom_call_target="tpu_custom_call" | custom-call | tf_op jit(solution)/shard_map/pallas_call | solution.py:558
  81.9 35.2 %shard_map.87 = (f32[2,2,512,512]{3,2,1,0:T(8,128)}, f32[2,2,768,256]{3,2,1,0:T(8,128)}, f32[2,2,256,512]{3,2,1,0:T(8,128)}, f32[2,256,256]{2,1,0:T(8,128)}) custom-call(s32[8]{0:T(128)} %get-tuple-element.31.row_offsets, s32[8]{0:T(128)} %get-tuple-element.30.column_offsets, s32[1]{0:T(128)} %bitcast.1.count, s32[8]{0:T(128)} %get-tuple-element.29.owners, ...), custom_call_target="tpu_custom_call" | custom-call | flops 12884901888 | bytes 33554432 | tf_op jit(solution)/shard_map/pallas_call | solution.py:306
  117.1 84.7 %shard_map.88 = (f32[2,2,512,256]{3,2,1,0:T(8,128)}, f32[2,2,256,512]{3,2,1,0:T(8,128)}, f32[512,256]{1,0:T(8,128)}) custom-call(f32[2,2,768,256]{3,2,1,0:T(8,128)} %get-tuple-element.18.all_right, f32[2,2,256,512]{3,2,1,0:T(8,128)} %get-tuple-element.19.all_lower, f32[512,256]{1,0:T(8,128)} %bitcast.8, f32[512,256]{1,0:T(8,128)} %bitcast.7), custom_call_target="tpu_custom_call" | custom-call | tf_op jit(solution)/shard_map/pallas_call | solution.py:711
  201.8 0.0 copy-start
  201.8 5.9 %shard_map.89 = f32[2,2,512,512]{3,2,1,0:T(8,128)} custom-call(f32[2,2,512,512]{3,2,1,0:T(8,128)} %get-tuple-element.17.moved, f32[2,2,512,256]{3,2,1,0:T(8,128)} %get-tuple-element.21.right, f32[2,2,256,512]{3,2,1,0:T(8,128)} %get-tuple-element.22.lower), custom_call_target="tpu_custom_call" | custom-call | flops 3145728 | bytes 12582912 | tf_op jit(solution)/shard_map/pallas_call | solution.py:345
  207.7 0.0 copy-done
  207.7 0.8 copy.13
  (3 shorter events, 0.0 us)
Async XLA Ops:
  201.8 5.9 %copy-start = (f32[512,256]{1,0:T(8,128)S(1)}, f32[512,256]{1,0:T(8,128)}, u32[]{:S(2)}) copy-start(f32[512,256]{1,0:T(8,128)} %get-tuple-element.23) | copy-start | bytes 1572868

commit v6 on v5

--- a/solution.py
+++ b/solution.py
@@ -394,9 +394,9 @@
 
 
 def pass_on(routes, paths, down):
-    for number in range(len(routes[0])):
+    for number in range(HOPS):
         for route, path in zip(routes, paths):
-            for hop in range(1, len(path) - 1):
+            for hop in range(1, len(path) - 1 if number < len(route) else 0):
                 when(down == path[hop], route[number][hop - 1].wait_recv)
                 when(down == path[hop], route[number][hop].start)
 
@@ -626,14 +626,16 @@
     pieces = [pl.ds(piece * chunk, chunk) for piece in range(HOPS)]
     routes = []
     at = base + 4 * layers
-    for number, (path, layer) in enumerate(zip(paths, (last, first, last))):
-        if number == 0:
-            sources, lanes = [held.at[layer, :, piece, :] for piece in pieces], start
-        else:
-            sources, lanes = [lowers[layer].at[:, piece, rest] for piece in pieces], rest
+    straight = (half - 1, half)
+    plan = ((paths[0], last, start, 0, HOPS, 0), (paths[1], first, rest, 0, 3, 1), (straight, first, rest, 3, HOPS, 1),
+            (paths[2], last, rest, 0, 3, 2), (straight, last, rest, 3, HOPS, 2))
+    paths = [path for path, *_ in plan]
+    for path, layer, span, begin, end, number in plan:
+        held_rows = held.at[layer] if number == 0 else lowers[layer].at[:, :, span]
         routes.append(detour(
-            path, along, sources, [lower_in.at[layer, :, piece, lanes] for piece in pieces], relay.at[number], send_sems, recv_sems, at))
-        at += HOPS * (len(path) - 1)
+            path, along, [held_rows.at[:, piece, :] for piece in pieces[begin:end]],
+            [lower_in.at[layer, :, piece, span] for piece in pieces[begin:end]], relay.at[number], send_sems, recv_sems, at))
+        at += (end - begin) * (len(path) - 1)
     for layer in range(layers):
         when(not_bottom & not_last, corners[layer].start)
 

time: 209 us -> 203 us (0.971); the launches traced: 208 us -> 199 us
  Pallas kernels: 202 us -> 193 us
    pallas_call x1, Pallas kernels: 84.7 us -> 75.8 us  [send_back(): pl.pallas_call(functools.partial(return_kernel, scale), out_shape=[shape(...]
where the time goes in v6:
time: 203 us; the launch traced here: 199 us
  Pallas kernels  193 us (95%)
  other arithmetic  3.15 us (2%)
  local copies, waits for them, and re-layouts  2.58 us (1%)
    pallas_call x1, Pallas kernels, fetch(): pl.pallas_call(fetch_kernel, out_shape=[shape(layers, 2, rows, points), s...  76.3 us
    pallas_call x1, Pallas kernels, send_back(): pl.pallas_call(functools.partial(return_kernel, scale), out_shape=[shape(...  75.8 us
    pallas_call x1, Pallas kernels, gradients(): pl.pallas_call(gradient_kernel, out_shape=[shape(*object_slab.shape), sha...  35.1 us
    pallas_call x1, Pallas kernels, finish(): pl.pallas_call(finish_kernel, out_shape=jax.ShapeDtypeStruct(moved.shape,...  5.88 us

profile of v6, /device:TPU:104, one launch (start us, length us, event | category | flops | bytes accessed | tf_op | source)
XLA Modules:
  0.0 199.5 jit_solution(13687361778124888886)
XLA Ops:
  0.6 1.3 convert_reduce_fusion.1
  2.0 0.1 pad_add_fusion
  2.1 0.8 reshape.58
  2.8 0.7 select_reduce_fusion.source
  3.5 0.8 slice_reduce_fusion
  4.3 0.1 reshape_squeeze.7
  4.4 0.1 reshape_squeeze.6
  4.5 0.2 select_reduce_fusion.1
  4.6 0.1 copy.11
  4.7 0.1 add_reduce_fusion
  4.9 0.7 fusion.2
  5.6 76.3 %shard_map.86 = (f32[2,2,512,256]{3,2,1,0:T(8,128)}, f32[2,2,256,512]{3,2,1,0:T(8,128)}, f32[2,2,256,256]{3,2,1,0:T(8,128)}, f32[16,256,256]{2,1,0:T(8,128)}) custom-call(s32[32]{0:T(128)} %select_reduce_fusion.source, f32[48,256,256]{2,1,0:T(8,128)} %frames.1, f32[2,2,512,512]{3,2,1,0:T(8,128)} %slab.3), custom_call_target="tpu_custom_call" | custom-call | tf_op jit(solution)/shard_map/pallas_call | solution.py:558
  81.9 35.1 %shard_map.87 = (f32[2,2,512,512]{3,2,1,0:T(8,128)}, f32[2,2,768,256]{3,2,1,0:T(8,128)}, f32[2,2,256,512]{3,2,1,0:T(8,128)}, f32[2,256,256]{2,1,0:T(8,128)}) custom-call(s32[8]{0:T(128)} %get-tuple-element.31.row_offsets, s32[8]{0:T(128)} %get-tuple-element.30.column_offsets, s32[1]{0:T(128)} %bitcast.1.count, s32[8]{0:T(128)} %get-tuple-element.29.owners, ...), custom_call_target="tpu_custom_call" | custom-call | flops 12884901888 | bytes 33554432 | tf_op jit(solution)/shard_map/pallas_call | solution.py:306
  117.0 75.8 %shard_map.88 = (f32[2,2,512,256]{3,2,1,0:T(8,128)}, f32[2,2,256,512]{3,2,1,0:T(8,128)}, f32[512,256]{1,0:T(8,128)}) custom-call(f32[2,2,768,256]{3,2,1,0:T(8,128)} %get-tuple-element.18.all_right, f32[2,2,256,512]{3,2,1,0:T(8,128)} %get-tuple-element.19.all_lower, f32[512,256]{1,0:T(8,128)} %bitcast.8, f32[512,256]{1,0:T(8,128)} %bitcast.7), custom_call_target="tpu_custom_call" | custom-call | tf_op jit(solution)/shard_map/pallas_call | solution.py:713
  192.8 0.0 copy-start
  192.8 5.9 %shard_map.89 = f32[2,2,512,512]{3,2,1,0:T(8,128)} custom-call(f32[2,2,512,512]{3,2,1,0:T(8,128)} %get-tuple-element.17.moved, f32[2,2,512,256]{3,2,1,0:T(8,128)} %get-tuple-element.21.right, f32[2,2,256,512]{3,2,1,0:T(8,128)} %get-tuple-element.22.lower), custom_call_target="tpu_custom_call" | custom-call | flops 3145728 | bytes 12582912 | tf_op jit(solution)/shard_map/pallas_call | solution.py:345
  198.7 0.0 copy-done
  198.7 0.8 copy.13
  (3 shorter events, 0.0 us)
Async XLA Ops:
  192.8 5.9 %copy-start = (f32[512,256]{1,0:T(8,128)S(1)}, f32[512,256]{1,0:T(8,128)}, u32[]{:S(2)}) copy-start(f32[512,256]{1,0:T(8,128)} %get-tuple-element.23) | copy-start | bytes 1572868

commit v7 on v6

--- a/solution.py
+++ b/solution.py
@@ -12,7 +12,7 @@
 
 MESH = pl.DeviceIdType.MESH
 TILE_CAP = 8
-HOPS = 4
+HOPS = 8
 PAIR = 2
 EARLY_FRAMES = (12, 14)
 BACKGROUND = 0.5
@@ -627,8 +627,8 @@
     routes = []
     at = base + 4 * layers
     straight = (half - 1, half)
-    plan = ((paths[0], last, start, 0, HOPS, 0), (paths[1], first, rest, 0, 3, 1), (straight, first, rest, 3, HOPS, 1),
-            (paths[2], last, rest, 0, 3, 2), (straight, last, rest, 3, HOPS, 2))
+    plan = ((paths[0], last, start, 0, HOPS, 0), (paths[1], first, rest, 0, 6, 1), (straight, first, rest, 6, HOPS, 1),
+            (paths[2], last, rest, 0, 6, 2), (straight, last, rest, 6, HOPS, 2))
     paths = [path for path, *_ in plan]
     for path, layer, span, begin, end, number in plan:
         held_rows = held.at[layer] if number == 0 else lowers[layer].at[:, :, span]

time: 203 us -> 203 us (level)
  the two profiles are of different devices: /device:TPU:104 before, /device:TPU:1 now
where the time goes in v7:
time: 203 us; the launch traced here: 201 us
  Pallas kernels  194 us (96%)
  other arithmetic  3.15 us (2%)
  local copies, waits for them, and re-layouts  2.58 us (1%)
    pallas_call x1, Pallas kernels, send_back(): pl.pallas_call(functools.partial(return_kernel, scale), out_shape=[shape(...  77.3 us
    pallas_call x1, Pallas kernels, fetch(): pl.pallas_call(fetch_kernel, out_shape=[shape(layers, 2, rows, points), s...  75.7 us
    pallas_call x1, Pallas kernels, gradients(): pl.pallas_call(gradient_kernel, out_shape=[shape(*object_slab.shape), sha...  35.4 us
    pallas_call x1, Pallas kernels, finish(): pl.pallas_call(finish_kernel, out_shape=jax.ShapeDtypeStruct(moved.shape,...  5.77 us

profile of v7, /device:TPU:1, one launch (start us, length us, event | category | flops | bytes accessed | tf_op | source)
XLA Modules:
  0.0 200.6 jit_solution(2356192416686217226)
XLA Ops:
  0.6 1.3 convert_reduce_fusion.1
  2.0 0.1 pad_add_fusion
  2.1 0.8 reshape.58
  2.8 0.7 select_reduce_fusion.source
  3.5 0.8 slice_reduce_fusion
  4.3 0.1 reshape_squeeze.7
  4.4 0.1 reshape_squeeze.6
  4.5 0.2 select_reduce_fusion.1
  4.6 0.1 copy.11
  4.7 0.1 add_reduce_fusion
  4.9 0.7 fusion.2
  5.6 75.7 %shard_map.86 = (f32[2,2,512,256]{3,2,1,0:T(8,128)}, f32[2,2,256,512]{3,2,1,0:T(8,128)}, f32[2,2,256,256]{3,2,1,0:T(8,128)}, f32[16,256,256]{2,1,0:T(8,128)}) custom-call(s32[32]{0:T(128)} %select_reduce_fusion.source, f32[48,256,256]{2,1,0:T(8,128)} %frames.1, f32[2,2,512,512]{3,2,1,0:T(8,128)} %slab.3), custom_call_target="tpu_custom_call" | custom-call | tf_op jit(solution)/shard_map/pallas_call | solution.py:558
  81.3 35.4 %shard_map.87 = (f32[2,2,512,512]{3,2,1,0:T(8,128)}, f32[2,2,768,256]{3,2,1,0:T(8,128)}, f32[2,2,256,512]{3,2,1,0:T(8,128)}, f32[2,256,256]{2,1,0:T(8,128)}) custom-call(s32[8]{0:T(128)} %get-tuple-element.31.row_offsets, s32[8]{0:T(128)} %get-tuple-element.30.column_offsets, s32[1]{0:T(128)} %bitcast.1.count, s32[8]{0:T(128)} %get-tuple-element.29.owners, ...), custom_call_target="tpu_custom_call" | custom-call | flops 12884901888 | bytes 33554432 | tf_op jit(solution)/shard_map/pallas_call | solution.py:306
  116.7 77.3 %shard_map.88 = (f32[2,2,512,256]{3,2,1,0:T(8,128)}, f32[2,2,256,512]{3,2,1,0:T(8,128)}, f32[512,256]{1,0:T(8,128)}) custom-call(f32[2,2,768,256]{3,2,1,0:T(8,128)} %get-tuple-element.18.all_right, f32[2,2,256,512]{3,2,1,0:T(8,128)} %get-tuple-element.19.all_lower, f32[512,256]{1,0:T(8,128)} %bitcast.8, f32[512,256]{1,0:T(8,128)} %bitcast.7), custom_call_target="tpu_custom_call" | custom-call | tf_op jit(solution)/shard_map/pallas_call | solution.py:713
  194.0 0.0 copy-start
  194.0 5.8 %shard_map.89 = f32[2,2,512,512]{3,2,1,0:T(8,128)} custom-call(f32[2,2,512,512]{3,2,1,0:T(8,128)} %get-tuple-element.17.moved, f32[2,2,512,256]{3,2,1,0:T(8,128)} %get-tuple-element.21.right, f32[2,2,256,512]{3,2,1,0:T(8,128)} %get-tuple-element.22.lower), custom_call_target="tpu_custom_call" | custom-call | flops 3145728 | bytes 12582912 | tf_op jit(solution)/shard_map/pallas_call | solution.py:345
  199.8 0.0 copy-done
  199.8 0.8 copy.13
  (3 shorter events, 0.0 us)
Async XLA Ops:
  194.0 5.8 %copy-start = (f32[512,256]{1,0:T(8,128)S(1)}, f32[512,256]{1,0:T(8,128)}, u32[]{:S(2)}) copy-start(f32[512,256]{1,0:T(8,128)} %get-tuple-element.23) | copy-start | bytes 1572868
